TPU v7x, 32 devices: a whole 2x2x4 slice. The times are simulated.
32 devices in a mesh: tile: 8 (over z, x), pos: 4 (over y, core).
Axes of the slice: x: 2, y: 2, z: 4, core: 2. Of those that a mesh axis runs over, the one named last changes fastest.
Arguments:
- obj_real: float32 [4, 2048, 256], P(None, ('tile', 'pos')), may hold values from 0.5 to 1.5
- obj_imag: float32 [4, 2048, 256], P(None, ('tile', 'pos')), may hold values from -4 to 4
- probe: float32 [2, 128, 128], replicated, may hold values from -6 to 6
- fresnel_phase: float32 [33], replicated, may hold values from -3.140625 to 3.140625
- row_offset: int32 [512], P('tile'), may hold values from 0 to 255
- col_offset: int32 [512], P('tile'), may hold values from 0 to 128
- live_count: int32 [8], P('tile'), may hold values from 16 to 64, as said below
- measured: bfloat16 [512, 128, 128], P('tile'), may hold values from 0.19921875 to 2
Outputs:
- grad_real: float32 [4, 2048, 256], P(None, ('tile', 'pos'))
- grad_imag: float32 [4, 2048, 256], P(None, ('tile', 'pos'))
Inputs may be any that keep to these rules, and one draw needn't show every extreme that they name: `row_offset`: row offsets count from the first of the 256 rows of the position's band. Band g uses its first live_count[g] slots; some band uses all 64.
All inputs are finite; a program needn't handle non-finite values.
Results may differ from a plain program's by a relative error of at most 0.012.
The roundings to bfloat16 on the way count: a program that leaves them out, or rounds other values in their place, can miss the bound.
Values sent between devices are 32-bit elements; how exact they have to be, the bound alone decides.
A program may use at most 64 MiB of HBM per device.

v0:
```python
import jax
import jax.numpy as jnp
from jax import lax
from jax.sharding import PartitionSpec as P

AMP_FLOOR = 0.25


def from_behind(value, axis, steps):
    count = lax.axis_size(axis)
    leading, last = (max(0, -steps), min(count, count - steps))
    return lax.ppermute(value, axis, [(source, source + steps) for source in range(leading, last)])


def half_dot(left, right):
    return jnp.dot(
        left.astype(jnp.bfloat16), right.astype(jnp.bfloat16), preferred_element_type=jnp.float32
    )


def complex_dot(left, right):
    real = half_dot(left[0], right[0]) - half_dot(left[1], right[1])
    imag = half_dot(left[0], right[1]) + half_dot(left[1], right[0])
    return (real, imag)


def two_sided(matrix, wave):
    inner = complex_dot(matrix, wave)
    return complex_dot(inner, (matrix[0].T, matrix[1].T))


def tables(phase, patch):
    taps = phase.shape[0]
    rows = jnp.arange(patch, dtype=jnp.int32)[:, None]
    cols = jnp.arange(patch, dtype=jnp.int32)[None, :]
    offset = cols - rows + taps // 2
    picked = (offset[:, :, None] == jnp.arange(taps, dtype=jnp.int32)[None, None, :]).astype(
        phase.dtype
    )
    scale = 1.0 / jnp.sqrt(jnp.asarray(taps, phase.dtype))
    kern_re = (jnp.sum(picked * jnp.cos(phase), axis=-1) * scale).astype(jnp.bfloat16)
    kern_im = (jnp.sum(picked * jnp.sin(phase), axis=-1) * scale).astype(jnp.bfloat16)
    product = rows * cols % patch
    angle = 2.0 * jnp.pi / patch * product.astype(phase.dtype)
    norm = 1.0 / jnp.sqrt(jnp.asarray(patch, phase.dtype))
    dft_re = (jnp.cos(angle) * norm).astype(jnp.bfloat16)
    dft_im = (-jnp.sin(angle) * norm).astype(jnp.bfloat16)
    return ((kern_re, kern_im), (dft_re, dft_im))


def exit_loss(piece_re, piece_im, probe, target, weight, kernel, dft):
    wave_re, wave_im = (probe[0], probe[1])
    slices = piece_re.shape[0]
    for layer in range(slices):
        o_re, o_im = (piece_re[layer], piece_im[layer])
        wave_re, wave_im = (wave_re * o_re - wave_im * o_im, wave_re * o_im + wave_im * o_re)
        if layer + 1 < slices:
            wave_re, wave_im = two_sided(kernel, (wave_re, wave_im))
    far_re, far_im = two_sided(dft, (wave_re, wave_im))
    amplitude = jnp.sqrt(far_re * far_re + far_im * far_im + AMP_FLOOR)
    return 0.5 * weight * jnp.sum((amplitude - target) ** 2)


def local(obj_real, obj_imag, probe, fresnel_phase, row_offset, col_offset, live_count, measured):
    slices, band, width = obj_real.shape
    members = lax.axis_size("pos")
    patch = probe.shape[-1]
    capacity = row_offset.shape[0]
    whole_re, whole_im = (
        lax.all_gather(obj_real, "pos", axis=1, tiled=True),
        lax.all_gather(obj_imag, "pos", axis=1, tiled=True),
    )
    next_re, next_im = from_behind((whole_re, whole_im), "tile", -1)
    ext_re = jnp.concatenate([whole_re, next_re], axis=1)
    ext_im = jnp.concatenate([whole_im, next_im], axis=1)
    rows = whole_re.shape[1]
    kernel, dft = tables(fresnel_phase, patch)
    member = lax.axis_index("pos")
    live = live_count[0]
    zero = jnp.zeros((), jnp.int32)
    grad_many = jax.vmap(
        jax.grad(exit_loss, argnums=(0, 1)), in_axes=(0, 0, None, 0, 0, None, None)
    )

    def cut(field, top, left):
        return lax.dynamic_slice(field, (zero, top, left), (slices, patch, patch))

    slots = member + members * jnp.arange(capacity // members, dtype=jnp.int32)
    tops = jnp.take(row_offset, slots, axis=0)
    lefts = jnp.take(col_offset, slots, axis=0)
    targets = jnp.take(measured, slots, axis=0).astype(jnp.float32)
    weights = (slots < live).astype(jnp.float32)
    pieces_re = jax.vmap(cut, in_axes=(None, 0, 0))(ext_re, tops, lefts)
    pieces_im = jax.vmap(cut, in_axes=(None, 0, 0))(ext_im, tops, lefts)
    grads_re, grads_im = grad_many(pieces_re, pieces_im, probe, targets, weights, kernel, dft)

    def add_one(carry, item):
        top, left, one_re, one_im = item
        acc_re = lax.dynamic_update_slice(
            carry[0], cut(carry[0], top, left) + one_re, (zero, top, left)
        )
        acc_im = lax.dynamic_update_slice(
            carry[1], cut(carry[1], top, left) + one_im, (zero, top, left)
        )
        return ((acc_re, acc_im), None)

    start = (jnp.zeros_like(ext_re), jnp.zeros_like(ext_im))
    (acc_re, acc_im), _ = lax.scan(add_one, start, (tops, lefts, grads_re, grads_im))
    spill_re, spill_im = from_behind((acc_re[:, rows:], acc_im[:, rows:]), "tile", 1)
    out_re, out_im = (
        lax.psum_scatter(acc_re[:, :rows] + spill_re, "pos", scatter_dimension=1, tiled=True),
        lax.psum_scatter(acc_im[:, :rows] + spill_im, "pos", scatter_dimension=1, tiled=True),
    )
    return (out_re, out_im)


def solution(mesh):
    in_specs = (
        P(None, ("tile", "pos"), None),
        P(None, ("tile", "pos"), None),
        P(),
        P(),
        P("tile"),
        P("tile"),
        P("tile"),
        P("tile", None, None),
    )
    out_specs = (P(None, ("tile", "pos"), None), P(None, ("tile", "pos"), None))
    return jax.shard_map(local, mesh=mesh, in_specs=in_specs, out_specs=out_specs, check_vma=False)
```

profile of v0, /device:TPU:16, one launch (start us, length us, event | category | flops | bytes accessed | tf_op | source)
XLA Modules:
  0.0 566.4 jit_solution(1097361584142550157)
XLA Ops:
  12.1 15.3 %all-gather.3.cloned.1.call-done = f32[4,256,256]{2,1,0:T(8,128)} async-done(((f32[4,64,256]{2,1,0:T(8,128)}), f32[4,256,256]{2,1,0:T(8,128)}) %all-gather.3.cloned.1.call-update) | async-done | bytes 1048592 | tf_op jit(solution)/shard_map/all_gather | solution.py:70
  33.5 12.2 %all-gather.5.cloned.1.call-done = f32[4,256,256]{2,1,0:T(8,128)} async-done(((f32[4,64,256]{2,1,0:T(8,128)}), f32[4,256,256]{2,1,0:T(8,128)}) %all-gather.5.cloned.1.call-update) | async-done | bytes 1048592 | tf_op jit(solution)/shard_map/all_gather | solution.py:71
  49.1 6.5 %collective-permute-done = f32[4,256,256]{2,1,0:T(8,128)} collective-permute-done((f32[4,256,256]{2,1,0:T(8,128)}, f32[4,256,256]{2,1,0:T(8,128)}, u32[]{:S(2)}, u32[]{:S(2)}) %collective-permute-start) | collective-permute-done | bytes 1048608 | tf_op jit(solution)/shard_map/ppermute | solution.py:12
  61.1 59.9 %while.15 = (s32[]{:T(128)}, f32[4,512,256]{2,1,0:T(8,128)}, s32[16,3]{0,1:T(4,128)S(1)}, f32[16,4,128,128]{3,2,0,1:T(8,128)}, s32[]{:T(128)}) while((s32[]{:T(128)}, f32[4,512,256]{2,1,0:T(8,128)}, s32[16,3]{0,1:T(4,128)S(1)}, f32[16,4,128,128]{3,2,0,1:T(8,128)}, s32[]{:T(128)}) %tuple.86), condition=%wide.while_cond, body=%wide.while_body.sunk | while | flops 2 | bytes 525929 | solution.py:86
  126.2 62.0 %while.16 = (s32[]{:T(128)}, f32[4,512,256]{2,1,0:T(8,128)}, s32[16,3]{0,1:T(4,128)S(1)}, f32[16,4,128,128]{3,2,0,1:T(8,128)}, s32[]{:T(128)}) while((s32[]{:T(128)}, f32[4,512,256]{2,1,0:T(8,128)}, s32[16,3]{0,1:T(4,128)S(1)}, f32[16,4,128,128]{3,2,0,1:T(8,128)}, s32[]{:T(128)}) %tuple.100), condition=%wide.while_cond.1, body=%wide.while_body.1.sunk | while | flops 2 | bytes 525929 | solution.py:86
  229.3 246.7 %while.14 = (s32[]{:T(128)}, f32[4,512,256]{2,1,0:T(8,128)}, f32[4,512,256]{2,1,0:T(8,128)}, s32[16]{0:T(128)S(1)}, s32[16]{0:T(128)S(1)}, /*index=5*/f32[16,4,1...) while((s32[]{:T(128)}, f32[4,512,256]{2,1,0:T(8,128)}, ...), condition=%wide.region_3.5_spmd, body=%wide.region_2.4_spmd.sunk | while | flops 131080 | bytes 2621661 | solution.py:108
  236.0 4.4 dynamic_update_slice.9
  240.3 4.4 dynamic_update_slice.8
  251.4 4.4 dynamic_update_slice.9
  255.8 4.4 dynamic_update_slice.8
  282.2 4.4 dynamic_update_slice.9
  297.6 4.4 dynamic_update_slice.9
  301.9 4.4 dynamic_update_slice.8
  328.3 4.4 dynamic_update_slice.9
  343.7 4.4 dynamic_update_slice.9
  359.1 4.4 dynamic_update_slice.9
  363.5 4.4 dynamic_update_slice.8
  374.5 4.4 dynamic_update_slice.9
  378.9 4.4 dynamic_update_slice.8
  390.0 4.4 dynamic_update_slice.9
  394.4 4.4 dynamic_update_slice.8
  405.5 4.4 dynamic_update_slice.9
  409.8 4.4 dynamic_update_slice.8
  420.9 4.4 dynamic_update_slice.9
  440.7 4.4 dynamic_update_slice.8
  451.7 4.4 dynamic_update_slice.9
  456.1 4.4 dynamic_update_slice.8
  467.2 4.4 dynamic_update_slice.9
  471.6 4.4 dynamic_update_slice.8
  481.5 22.2 %collective-permute-done.3 = f32[4,256,256]{2,1,0:T(8,128)S(1)} collective-permute-done((f32[4,256,256]{2,1,0:T(8,128)S(1)}, f32[4,256,256]{2,1,0:T(8,128)S(1)}, u32[]{:S(2)}, u32[]{:S(2)}) %collective-permute-start.3) | collective-permute-done | bytes 1048608 | tf_op jit(solution)/shard_map/ppermute | solution.py:12
  510.7 22.3 %collective-permute-done.2 = f32[4,256,256]{2,1,0:T(8,128)S(1)} collective-permute-done((f32[4,256,256]{2,1,0:T(8,128)S(1)}, f32[4,256,256]{2,1,0:T(8,128)S(1)}, u32[]{:S(2)}, u32[]{:S(2)}) %collective-permute-start.2) | collective-permute-done | bytes 1048608 | tf_op jit(solution)/shard_map/ppermute | solution.py:12
  535.4 24.4 %reduce-scatter.3.cloned.1.call-done = f32[4,64,256]{2,1,0:T(8,128)} async-done(((f32[4,256,256]{2,1,0:T(8,128)}), f32[4,64,256]{2,1,0:T(8,128)}) %reduce-scatter.3.cloned.1.call-update) | async-done | bytes 262160 | tf_op jit(solution)/shard_map/reduce_scatter | solution.py:111
  (274 shorter events, 285.2 us)
Async XLA Ops:
  7.2 23.6 %copy-start = (bf16[64,128,128]{2,1,0:T(8,128)(2,1)S(1)}, bf16[64,128,128]{2,1,0:T(8,128)(2,1)}, u32[]{:S(2)}) copy-start(bf16[64,128,128]{2,1,0:T(8,128)(2,1)} %param.19) | copy-start | bytes 6291460
  7.2 20.2 %all-gather.3.cloned.1.call-start = ((), (), s32[]{:S(2)}) async-start(), calls=%async_computation.2 | async-start | bytes 1310720 | tf_op jit(solution)/shard_map/all_gather | solution.py:70
  7.9 37.8 %all-gather.5.cloned.1.call-start = ((), (), s32[]{:S(2)}) async-start(), calls=%async_computation.3 | async-start | bytes 1310720 | tf_op jit(solution)/shard_map/all_gather | solution.py:71
  8.7 526.8 %reduce-scatter.5.cloned.1.call-start = ((), (), s32[]{:S(2)}) async-start(), calls=%async_computation.5 | async-start | bytes 1310720 | tf_op jit(solution)/shard_map/reduce_scatter | solution.py:112
  27.4 28.2 %collective-permute-start = (f32[4,256,256]{2,1,0:T(8,128)}, f32[4,256,256]{2,1,0:T(8,128)}, u32[]{:S(2)}, u32[]{:S(2)}) collective-permute-start(f32[4,256,256]{2,1,0:T(8,128)} %all-gather.3.cloned.1.call-done), channel_id=1, source_target_pairs={{4,0},{8,4},{12,8},{16,12},{20,16},{24,20},{28,24},{5,1},{9,5},{13... | collective-permute-start | bytes 3145736 | tf_op jit(solution)/shard_map/ppermute | solution.py:12
  45.7 75.3 %collective-permute-start.1 = (f32[4,256,256]{2,1,0:T(8,128)}, f32[4,256,256]{2,1,0:T(8,128)}, u32[]{:S(2)}, u32[]{:S(2)}) collective-permute-start(f32[4,256,256]{2,1,0:T(8,128)} %all-gather.5.cloned.1.call-done), channel_id=1, source_target_pairs={{4,0},{8,4},{12,8},{16,12},{20,16},{24,20},{28,24},{5,1},{9,5},{13... | collective-permute-start | bytes 3145736 | tf_op jit(solution)/shard_map/ppermute | solution.py:12
  58.6 62.3 %copy-start.4 = (f32[4,256,256]{2,1,0:T(8,128)S(1)}, f32[4,256,256]{2,1,0:T(8,128)}, u32[]{:S(2)}) copy-start(f32[4,256,256]{2,1,0:T(8,128)} %all-gather.5.cloned.1.call-done) | copy-start | bytes 3145732
  190.7 2.2 copy-start.3
  191.0 3.2 copy-start.2
  477.3 26.4 %collective-permute-start.3 = (f32[4,256,256]{2,1,0:T(8,128)S(1)}, f32[4,256,256]{2,1,0:T(8,128)S(1)}, u32[]{:S(2)}, u32[]{:S(2)}) collective-permute-start(f32[4,256,256]{2,1,0:T(8,128)S(1)} %slice.55), channel_id=1, source_target_pairs={{0,4},{4,8},{8,12},{12,16},{16,20},{20,24},{24,28},{1,5},{5,9},{9,... | collective-permute-start | bytes 3145736 | tf_op jit(solution)/shard_map/ppermute | solution.py:12
  503.7 56.2 %copy-start.1 = (bf16[64,128,128]{2,1,0:T(8,128)(2,1)S(1)}, bf16[64,128,128]{2,1,0:T(8,128)(2,1)}, u32[]{:S(2)}) copy-start(bf16[64,128,128]{2,1,0:T(8,128)(2,1)} %param.19) | copy-start | bytes 6291460
  506.2 53.7 %reduce-scatter.3.cloned.1.call-start = ((), (), s32[]{:S(2)}) async-start(), calls=%async_computation.4 | async-start | bytes 1310720 | tf_op jit(solution)/shard_map/reduce_scatter | solution.py:111
  507.6 25.5 %collective-permute-start.2 = (f32[4,256,256]{2,1,0:T(8,128)S(1)}, f32[4,256,256]{2,1,0:T(8,128)S(1)}, u32[]{:S(2)}, u32[]{:S(2)}) collective-permute-start(f32[4,256,256]{2,1,0:T(8,128)S(1)} %slice.53), channel_id=1, source_target_pairs={{0,4},{4,8},{8,12},{12,16},{16,20},{20,24},{24,28},{1,5},{5,9},{9,... | collective-permute-start | bytes 3145736 | tf_op jit(solution)/shard_map/ppermute | solution.py:12
Sparse Core Ops, SparseCore 0:
  9.6 17.7 all-gather.2
  29.0 16.7 all-gather.4
  506.3 23.8 reduce-scatter.4
  535.5 24.3 reduce-scatter.2
where the time goes:
time: 574 us; the launch traced here: 566 us
  local copies, waits for them, and re-layouts  298 us (52%)
  waiting for transfers between devices  104 us (18%)
  loops' own time  62.4 us (11%)
  other arithmetic  46.3 us (8%)
  matrix products  26 us (5%)
  between operations  15 us (3%)
  starting transfers between devices  14.2 us (2%)
    gather x96, local copies, waits for them, and re-layouts  122 us
    dynamic_update_slice x16, local copies, waits for them, and re-layouts, add_one(): lax.dynamic_update_slice(carry[1], cut(carry[1], top, left) + one_im, (ze...  70 us
    dynamic_update_slice x16, local copies, waits for them, and re-layouts, add_one(): lax.dynamic_update_slice(carry[0], cut(carry[0], top, left) + one_re, (ze...  69.9 us
    another operation x1, loops' own time, local(): lax.scan(add_one, start, (tops, lefts, grads_re, grads_im))  62.3 us
    ppermute x4, waiting for transfers between devices, from_behind(): lax.ppermute(value, axis, [(source, source + steps) for source in range(l...  51.1 us
    dot_general x64, matrix products, half_dot(): jnp.dot(left.astype(jnp.bfloat16), right.astype(jnp.bfloat16), preferred_...  26 us
    add x16, other arithmetic, add_one(): cut(carry[1], top, left) + one_im  25.7 us
    reduce_scatter x1, waiting for transfers between devices, local(): lax.psum_scatter(acc_re[:, :rows] + spill_re, 'pos', scatter_dimension=1,...  24.4 us
  transfers between devices with their start and end apart: 8, of which 6 were waited for; matrix products, arithmetic and copies ran while one was open for 13% of the time, Pallas kernels for 0%

commit v1 on v0

v1 whole, which is shorter than its diff:
```python
import functools

import jax
import jax.numpy as jnp
import ml_dtypes
import numpy as np
from jax import lax
from jax.experimental import pallas as pl
from jax.experimental.pallas import tpu as pltpu
from jax.sharding import PartitionSpec as P

AMP_FLOOR = 0.25
BATCH = 4


def dft_tables(patch):
    grid = np.arange(patch)
    product = (grid[:, None] * grid[None, :] % patch).astype(np.float32)
    angle = np.float32(2.0 * np.pi / patch) * product
    norm = np.float32(1.0) / np.sqrt(np.float32(patch))
    real = (np.cos(angle) * norm).astype(ml_dtypes.bfloat16)
    imag = (-np.sin(angle) * norm).astype(ml_dtypes.bfloat16)
    left = np.block([[real, -imag], [imag, real]])
    right = np.block([[real.T, imag.T], [-imag.T, real.T]])
    return jnp.asarray(left), jnp.asarray(right)


def dot(left, right):
    return jnp.dot(left, right, preferred_element_type=jnp.float32)


def stack_rows(pairs):
    return jnp.concatenate([jnp.concatenate(pair, axis=0) for pair in pairs], axis=1)


def stack_cols(pairs):
    return jnp.concatenate([jnp.concatenate(pair, axis=1) for pair in pairs], axis=0)


def split_rows(array, patch):
    count = array.shape[1] // patch
    return [
        (array[:patch, b * patch : (b + 1) * patch], array[patch:, b * patch : (b + 1) * patch])
        for b in range(count)
    ]


def split_cols(array, patch):
    count = array.shape[0] // patch
    return [
        (array[b * patch : (b + 1) * patch, :patch], array[b * patch : (b + 1) * patch, patch:])
        for b in range(count)
    ]


def halves(pairs):
    return [(a.astype(jnp.bfloat16), b.astype(jnp.bfloat16)) for a, b in pairs]


def forward_two_sided(left, right, pairs):
    patch = pairs[0][0].shape[0]
    inner = split_rows(dot(left, stack_rows(halves(pairs))), patch)
    return split_cols(dot(stack_cols(halves(inner)), right), patch)


def backward_two_sided(left, right, pairs):
    patch = pairs[0][0].shape[0]
    inner = split_cols(dot(stack_cols(halves(pairs)), left), patch)
    return split_rows(dot(right, stack_rows(halves(inner))), patch)


def compute_kernel(
    taps, rows_ref, cols_ref, live_ref, phase_ref, dft_left, dft_right, probe_ref,
    own_re, own_im, sib_re, sib_im, far_re, far_im, farsib_re, farsib_im, measured_ref,
    keep_ref, give_ref, spill_ref, spillgive_ref,
    window, acc, target, kern_left, kern_right, saved, patches, listed, in_sem, target_sem, out_sem,
):
    slices, shard, width = own_re.shape
    patch = probe_ref.shape[-1]
    slots = rows_ref.shape[0]
    parts = width // patch
    member = lax.axis_index("pos")
    pair, parity = member // 2, member % 2
    get_target = pltpu.make_async_copy(measured_ref, target, target_sem)
    get_target.start()
    loads = []
    sources = ((own_re, own_im), (sib_re, sib_im), (far_re, far_im), (farsib_re, farsib_im))
    spots = (parity, 1 - parity, 2 + parity, 3 - parity)
    for source, spot in zip(sources, spots):
        for part in range(2):
            for half in range(parts):
                loads.append(
                    pltpu.make_async_copy(
                        source[part].at[:, :, pl.ds(half * patch, patch)],
                        window.at[part, :, half, pl.ds(spot * shard, shard), :],
                        in_sem.at[len(loads)],
                    )
                )
    for load in loads:
        load.start()

    def pick(slot, count):
        ok = jnp.logical_and(slot < live_ref[0], rows_ref[slot] // (2 * shard) == pair)
        take = jnp.logical_and(ok, count % 2 == parity)
        listed[jnp.where(take, count // 2, slots)] = slot
        return count + ok.astype(jnp.int32)

    total = lax.fori_loop(0, slots, pick, jnp.int32(0))
    mine = (total + 1 - parity) // 2

    row = lax.broadcasted_iota(jnp.int32, (patch, patch), 0)
    col = lax.broadcasted_iota(jnp.int32, (patch, patch), 1)
    band = jnp.logical_and(col - row + taps // 2 >= 0, col - row + taps // 2 < taps)
    scale = 1.0 / jnp.sqrt(jnp.float32(taps))

    def toeplitz(values):
        wide = jnp.broadcast_to(values, (patch, patch))
        moved = pltpu.roll(wide, patch - taps // 2, 1, stride=1, stride_axis=0)
        return jnp.where(band, moved, 0.0)

    kern_re = toeplitz(jnp.cos(phase_ref[...]) * scale)
    kern_im = toeplitz(jnp.sin(phase_ref[...]) * scale)
    kern_left[...] = stack_rows(halves([(kern_re, kern_im), (-kern_im, kern_re)]))
    kern_re_t, kern_im_t = kern_re.T, kern_im.T
    kern_right[...] = stack_rows(halves([(kern_re_t, -kern_im_t), (kern_im_t, kern_re_t)]))
    acc[...] = jnp.zeros_like(acc)
    for load in loads:
        load.wait()
    get_target.wait()

    def group(step, carry):
        first = step * BATCH
        index = [listed[jnp.minimum(first + b, mine - 1)] for b in range(BATCH)]
        weight = [(first + b < mine).astype(jnp.float32) for b in range(BATCH)]
        top = [rows_ref[i] - pair * (2 * shard) for i in index]
        left = [cols_ref[i] for i in index]
        back = [(patch - x) % patch for x in left]
        forth = [x % patch for x in left]
        inside = [col >= x for x in left]

        def cut(layer, b, part):
            a0 = window[part, layer, 0, pl.ds(top[b], patch), :]
            a1 = window[part, layer, 1, pl.ds(top[b], patch), :]
            return pltpu.roll(jnp.where(inside[b], a0, a1), back[b], 1)

        waves = [(probe_ref[0], probe_ref[1]) for _ in range(BATCH)]
        for layer in range(slices):
            nxt = []
            for b in range(BATCH):
                o_re, o_im = cut(layer, b, 0), cut(layer, b, 1)
                w_re, w_im = waves[b]
                if layer:
                    patches[layer - 1, b, 0] = o_re
                    patches[layer - 1, b, 1] = o_im
                    saved[layer - 1, b, 0] = w_re
                    saved[layer - 1, b, 1] = w_im
                nxt.append((w_re * o_re - w_im * o_im, w_re * o_im + w_im * o_re))
            if layer + 1 < slices:
                waves = forward_two_sided(kern_left[...], kern_right[...], nxt)
            else:
                waves = forward_two_sided(dft_left[...], dft_right[...], nxt)
        grads = []
        for b in range(BATCH):
            f_re, f_im = waves[b]
            amplitude = jnp.sqrt(f_re * f_re + f_im * f_im + AMP_FLOOR)
            t = target[index[b]].astype(jnp.float32)
            ratio = weight[b] * (amplitude - t) / amplitude
            grads.append((f_re * ratio, f_im * ratio))
        grads = backward_two_sided(dft_left[...], dft_right[...], grads)
        for layer in reversed(range(slices)):
            nxt = []
            for b in range(BATCH):
                g_re, g_im = grads[b]
                if layer:
                    w_re, w_im = saved[layer - 1, b, 0], saved[layer - 1, b, 1]
                    o_re, o_im = patches[layer - 1, b, 0], patches[layer - 1, b, 1]
                    nxt.append((o_re * g_re + o_im * g_im, o_re * g_im - o_im * g_re))
                else:
                    w_re, w_im = probe_ref[0], probe_ref[1]
                terms = (w_re * g_re + w_im * g_im, w_re * g_im - w_im * g_re)
                for part in range(2):
                    moved = pltpu.roll(terms[part], forth[b], 1)
                    spot = pl.ds(top[b], patch)
                    acc[part, layer, 0, spot, :] += jnp.where(inside[b], moved, 0.0)
                    acc[part, layer, 1, spot, :] += jnp.where(inside[b], 0.0, moved)
            if layer:
                grads = backward_two_sided(kern_left[...], kern_right[...], nxt)
        return carry

    lax.fori_loop(0, (mine + BATCH - 1) // BATCH, group, 0)

    stores = []
    for result, spot in zip((keep_ref, give_ref, spill_ref, spillgive_ref), spots):
        for part in range(2):
            for half in range(parts):
                stores.append(
                    pltpu.make_async_copy(
                        acc.at[part, :, half, pl.ds(spot * shard, shard), :],
                        result.at[part, :, :, pl.ds(half * patch, patch)],
                        out_sem.at[len(stores)],
                    )
                )
    for store in stores:
        store.start()
    for store in stores:
        store.wait()


def local(obj_real, obj_imag, probe, fresnel_phase, row_offset, col_offset, live_count, measured):
    slices, shard, width = obj_real.shape
    patch = probe.shape[-1]
    members = lax.axis_size("pos")
    devices = lax.axis_size("tile") * members
    parts = width // patch
    taps = fresnel_phase.shape[0]
    both = ("tile", "pos")
    swap = [(d, d ^ 1) for d in range(members)]
    sib_re, sib_im = lax.ppermute((obj_real, obj_imag), "pos", swap)
    up = [(d, d - 2) for d in range(2, devices)]
    far_re, far_im = lax.ppermute((obj_real, obj_imag), both, up)
    farsib_re, farsib_im = lax.ppermute((far_re, far_im), "pos", swap)
    phase = jnp.pad(fresnel_phase, (0, patch - taps)).reshape(1, patch)
    dft_left, dft_right = dft_tables(patch)
    block = jax.ShapeDtypeStruct((2, slices, shard, width), jnp.float32)
    smem = pl.BlockSpec(memory_space=pltpu.SMEM)
    vmem = pl.BlockSpec(memory_space=pltpu.VMEM)
    anywhere = pl.BlockSpec(memory_space=pl.ANY)
    keep, give, spill, spillgive = pl.pallas_call(
        functools.partial(compute_kernel, taps),
        out_shape=[block] * 4,
        in_specs=[smem] * 3 + [vmem] * 4 + [anywhere] * 9,
        out_specs=[anywhere] * 4,
        scratch_shapes=[
            pltpu.VMEM((2, slices, parts, 4 * shard, patch), jnp.float32),
            pltpu.VMEM((2, slices, parts, 4 * shard, patch), jnp.float32),
            pltpu.VMEM(measured.shape, measured.dtype),
            pltpu.VMEM((2 * patch, 2 * patch), jnp.bfloat16),
            pltpu.VMEM((2 * patch, 2 * patch), jnp.bfloat16),
            pltpu.VMEM((slices - 1, BATCH, 2, patch, patch), jnp.float32),
            pltpu.VMEM((slices - 1, BATCH, 2, patch, patch), jnp.float32),
            pltpu.SMEM((row_offset.shape[0] + 8,), jnp.int32),
            pltpu.SemaphoreType.DMA((8 * parts,)),
            pltpu.SemaphoreType.DMA,
            pltpu.SemaphoreType.DMA((8 * parts,)),
        ],
        compiler_params=pltpu.CompilerParams(vmem_limit_bytes=40 * 1024 * 1024),
    )(
        row_offset, col_offset, live_count, phase, dft_left, dft_right, probe,
        obj_real, obj_imag, sib_re, sib_im, far_re, far_im, farsib_re, farsib_im, measured,
    )
    sib, spillsib = lax.ppermute((give, spillgive), "pos", swap)
    down = [(d, d + 2) for d in range(devices - 2)]
    behind = lax.ppermute(spill + spillsib, both, down)
    total = keep + sib + behind
    return total[0], total[1]


def solution(mesh):
    in_specs = (
        P(None, ("tile", "pos"), None),
        P(None, ("tile", "pos"), None),
        P(),
        P(),
        P("tile"),
        P("tile"),
        P("tile"),
        P("tile", None, None),
    )
    out_specs = (P(None, ("tile", "pos"), None), P(None, ("tile", "pos"), None))
    return jax.shard_map(local, mesh=mesh, in_specs=in_specs, out_specs=out_specs, check_vma=False)
```

time: 574 us -> 66.2 us (0.12); the launches traced: 566 us -> 66.3 us
  local copies, waits for them, and re-layouts: 298 us -> 9 us
  waiting for transfers between devices: 104 us -> 26 us
  loops' own time: 62.4 us -> 0 us
  other arithmetic: 46.3 us -> 0.2 us
  matrix products: 26 us -> 0 us
  Pallas kernels: 0 us -> 20 us
  between operations: 15 us -> 1.35 us
    dynamic_update_slice x32 -> x0, local copies, waits for them, and re-layouts: 140 us -> none  [the longest x16 70 us: add_one(): lax.dynamic_update_slice(carry[1], cut(carry[1], top, left) + one_im, (ze...]
    gather x99 -> x0, local copies, waits for them, and re-layouts: 125 us -> none
    another operation x3 -> x0, loops' own time: 62.4 us -> none  [the longest x1 62.3 us: local(): lax.scan(add_one, start, (tops, lefts, grads_re, grads_im))]
    add x19 -> x2, other arithmetic: 30.6 us -> 0.2 us  [the longest x1 0.11 us: local(): total = keep + sib + behind]
    all_gather x2 -> x0, waiting for transfers between devices: 27.5 us -> none  [the longest x1 15.3 us: local(): lax.all_gather(obj_real, 'pos', axis=1, tiled=True)]
    dot_general x64 -> x0, matrix products: 26 us -> none  [half_dot(): jnp.dot(left.astype(jnp.bfloat16), right.astype(jnp.bfloat16), preferred_...]
    ppermute x4 -> x9, waiting for transfers between devices: 51.1 us -> 26 us  [the longest x1 15.9 us: local(): behind = lax.ppermute(spill + spillsib, both, down)]
    reduce_scatter x2 -> x0, waiting for transfers between devices: 24.5 us -> none  [the longest x1 24.4 us: local(): lax.psum_scatter(acc_re[:, :rows] + spill_re, 'pos', scatter_dimension=1,...]
  transfers between devices with their start and end apart: 8 -> 9, of which waited for: 6 -> 5; matrix products, arithmetic and copies ran while one was open for 13% -> 1% of each run, Pallas kernels for 0% -> 0%
where the time goes in v1:
time: 66.2 us; the launch traced here: 66.3 us
  waiting for transfers between devices  26 us (39%)
  Pallas kernels  20 us (30%)
  starting transfers between devices  9.73 us (15%)
  local copies, waits for them, and re-layouts  9 us (14%)
  between operations  1.35 us (2%)
    pallas_call x1, Pallas kernels, local(): pl.pallas_call(functools.partial(compute_kernel, taps), out_shape=[block]...  20 us
    ppermute x1, waiting for transfers between devices, local(): behind = lax.ppermute(spill + spillsib, both, down)  15.9 us
    ppermute x2, waiting for transfers between devices, local(): far_re, far_im = lax.ppermute((obj_real, obj_imag), both, up)  8.51 us
    unnamed x16, local copies, waits for them, and re-layouts  7.51 us
    ppermute x2, starting transfers between devices, local(): far_re, far_im = lax.ppermute((obj_real, obj_imag), both, up)  6.66 us
    ppermute x1, starting transfers between devices, local(): behind = lax.ppermute(spill + spillsib, both, down)  1.92 us
    ppermute x2, waiting for transfers between devices, local(): sib, spillsib = lax.ppermute((give, spillgive), 'pos', swap)  1.4 us
  transfers between devices with their start and end apart: 9, of which 5 were waited for; matrix products, arithmetic and copies ran while one was open for 1% of the time, Pallas kernels for 0%

profile of v1, /device:TPU:16, one launch (start us, length us, event | category | flops | bytes accessed | tf_op | source)
XLA Modules:
  0.0 66.3 jit_solution(16844512134128211084)
XLA Ops:
  0.6 4.2 %collective-permute-start.2 = (f32[4,64,256]{2,1,0:T(8,128)}, f32[4,64,256]{2,1,0:T(8,128)S(1)}, u32[]{:S(2)}, u32[]{:S(2)}) collective-permute-start(f32[4,64,256]{2,1,0:T(8,128)} %own_re.1), channel_id=1, source_target_pairs={{2,0},{3,1},{4,2},{5,3},{6,4},{7,5},{8,6},{9,7},{10,8},{11,9},{12,... | collective-permute-start | bytes 786440 | tf_op jit(solution)/shard_map/ppermute | solution.py:220
  4.9 2.4 %collective-permute-start.3 = (f32[4,64,256]{2,1,0:T(8,128)}, f32[4,64,256]{2,1,0:T(8,128)S(1)}, u32[]{:S(2)}, u32[]{:S(2)}) collective-permute-start(f32[4,64,256]{2,1,0:T(8,128)} %own_im.1), channel_id=1, source_target_pairs={{2,0},{3,1},{4,2},{5,3},{6,4},{7,5},{8,6},{9,7},{10,8},{11,9},{12,... | collective-permute-start | bytes 786440 | tf_op jit(solution)/shard_map/ppermute | solution.py:220
  7.3 0.1 collective-permute-start
  7.4 0.5 collective-permute-start.1
  7.9 4.0 %collective-permute-done.2.far_re = f32[4,64,256]{2,1,0:T(8,128)S(1)} collective-permute-done((f32[4,64,256]{2,1,0:T(8,128)}, f32[4,64,256]{2,1,0:T(8,128)S(1)}, u32[]{:S(2)}, u32[]{:S(2)}) %collective-permute-start.2) | collective-permute-done | bytes 262176 | tf_op jit(solution)/shard_map/ppermute | solution.py:220
  11.9 0.0 collective-permute-start.4
  11.9 4.5 %collective-permute-done.3.far_im = f32[4,64,256]{2,1,0:T(8,128)S(1)} collective-permute-done((f32[4,64,256]{2,1,0:T(8,128)}, f32[4,64,256]{2,1,0:T(8,128)S(1)}, u32[]{:S(2)}, u32[]{:S(2)}) %collective-permute-start.3) | collective-permute-done | bytes 262176 | tf_op jit(solution)/shard_map/ppermute | solution.py:220
  16.4 0.0 collective-permute-start.5
  17.1 0.7 pad_bitcast_fusion.phase_ref
  17.7 0.0 collective-permute-done.sib_re
  17.7 0.0 collective-permute-done.1.sib_im
  17.7 0.0 collective-permute-done.4.farsib_re
  17.7 0.2 collective-permute-done.5.farsib_im
  17.9 0.0 copy-start
  17.9 1.6 %copy-done = bf16[64,128,128]{2,1,0:T(8,128)(2,1)S(1)} copy-done((bf16[64,128,128]{2,1,0:T(8,128)(2,1)S(1)}, bf16[64,128,128]{2,1,0:T(8,128)(2,1)}, u32[]{:S(2)}) %copy-start) | copy-done | bytes 2097176
  19.5 0.9 %copy-done.1 = f32[4,64,256]{2,1,0:T(8,128)S(1)} copy-done((f32[4,64,256]{2,1,0:T(8,128)S(1)}, f32[4,64,256]{2,1,0:T(8,128)}, u32[]{:S(2)}) %copy-start.1) | copy-done | bytes 262168
  20.5 0.9 %copy-done.2 = f32[4,64,256]{2,1,0:T(8,128)S(1)} copy-done((f32[4,64,256]{2,1,0:T(8,128)S(1)}, f32[4,64,256]{2,1,0:T(8,128)}, u32[]{:S(2)}) %copy-start.2) | copy-done | bytes 262168
  21.4 0.9 %copy-done.3 = f32[2,128,128]{2,1,0:T(8,128)S(1)} copy-done((f32[2,128,128]{2,1,0:T(8,128)S(1)}, f32[2,128,128]{2,1,0:T(8,128)}, u32[]{:S(2)}) %copy-start.3) | copy-done | bytes 131096
  22.3 0.9 %copy-done.4 = bf16[256,256]{1,0:T(8,128)(2,1)S(1)} copy-done((bf16[256,256]{1,0:T(8,128)(2,1)S(1)}, bf16[256,256]{1,0:T(8,128)(2,1)}, u32[]{:S(2)}) %copy-start.4) | copy-done | bytes 131096
  23.2 0.9 %copy-done.5 = bf16[256,256]{1,0:T(8,128)(2,1)S(1)} copy-done((bf16[256,256]{1,0:T(8,128)(2,1)S(1)}, bf16[256,256]{1,0:T(8,128)(2,1)}, u32[]{:S(2)}) %copy-start.5) | copy-done | bytes 131096
  24.1 0.7 copy-done.6
  24.8 0.7 copy-done.7
  25.5 20.0 %shard_map.113 = (f32[2,4,64,256]{3,2,1,0:T(8,128)S(1)}, f32[2,4,64,256]{3,2,1,0:T(8,128)S(1)}, f32[2,4,64,256]{3,2,1,0:T(8,128)S(1)}, f32[2,4,64,256]{3,2,1,0:T(8,128)S(1)}) custom-call(s32[64]{0:T(128)S(1)} %copy-done.6, s32[64]{0:T(128)S(1)} %copy-done.7, s32[1]{0:T(128)S(6)} %copy.12.live_ref, f32[1,128]{1,0:T(1,128)S(1)} %pad_bitcast_fusion.phase_ref, ...), custom_call_target="tpu_custom_call" | custom-call | tf_op jit(solution)/shard_map/pallas_call | solution.py:228
  45.5 0.4 collective-permute-start.7
  45.8 0.2 collective-permute-start.6
  46.1 1.4 %collective-permute-done.7 = f32[2,4,64,256]{3,2,1,0:T(8,128)S(1)} collective-permute-done((f32[2,4,64,256]{3,2,1,0:T(8,128)S(1)}, f32[2,4,64,256]{3,2,1,0:T(8,128)S(1)}, u32[]{:S(2)}, u32[]{:S(2)}) %collective-permute-start.7) | collective-permute-done | bytes 524320 | tf_op jit(solution)/shard_map/ppermute | solution.py:251
  47.5 0.1 add.12
  47.6 1.9 %collective-permute-start.8 = (f32[2,4,64,256]{3,2,1,0:T(8,128)S(1)}, f32[2,4,64,256]{3,2,1,0:T(8,128)S(1)}, u32[]{:S(2)}, u32[]{:S(2)}) collective-permute-start(f32[2,4,64,256]{3,2,1,0:T(8,128)S(1)} %add.12), channel_id=1, source_target_pairs={{0,2},{1,3},{2,4},{3,5},{4,6},{5,7},{6,8},{7,9},{8,10},{9,11},{10,... | collective-permute-start | bytes 1572872 | tf_op jit(solution)/shard_map/ppermute | solution.py:253
  49.5 0.0 collective-permute-done.6
  49.5 15.9 %collective-permute-done.8 = f32[2,4,64,256]{3,2,1,0:T(8,128)S(1)} collective-permute-done((f32[2,4,64,256]{3,2,1,0:T(8,128)S(1)}, f32[2,4,64,256]{3,2,1,0:T(8,128)S(1)}, u32[]{:S(2)}, u32[]{:S(2)}) %collective-permute-start.8) | collective-permute-done | bytes 524320 | tf_op jit(solution)/shard_map/ppermute | solution.py:253
  65.4 0.1 add_add_fusion
  65.5 0.8 %slice_bitcast_fusion = (f32[4,64,256]{2,1,0:T(8,128)}, f32[4,64,256]{2,1,0:T(8,128)}) fusion(f32[2,4,64,256]{3,2,1,0:T(8,128)S(1)} %add_add_fusion), kind=kLoop, calls=%fused_computation.1 | loop fusion | bytes 1048576 | tf_op jit(solution)/shard_map/squeeze | solution.py:255
  (7 shorter events, 0.0 us)
Async XLA Ops:
  0.6 11.3 %collective-permute-start.2 = (f32[4,64,256]{2,1,0:T(8,128)}, f32[4,64,256]{2,1,0:T(8,128)S(1)}, u32[]{:S(2)}, u32[]{:S(2)}) collective-permute-start(f32[4,64,256]{2,1,0:T(8,128)} %own_re.1), channel_id=1, source_target_pairs={{2,0},{3,1},{4,2},{5,3},{6,4},{7,5},{8,6},{9,7},{10,8},{11,9},{12,... | collective-permute-start | bytes 786440 | tf_op jit(solution)/shard_map/ppermute | solution.py:220
  4.9 11.5 %collective-permute-start.3 = (f32[4,64,256]{2,1,0:T(8,128)}, f32[4,64,256]{2,1,0:T(8,128)S(1)}, u32[]{:S(2)}, u32[]{:S(2)}) collective-permute-start(f32[4,64,256]{2,1,0:T(8,128)} %own_im.1), channel_id=1, source_target_pairs={{2,0},{3,1},{4,2},{5,3},{6,4},{7,5},{8,6},{9,7},{10,8},{11,9},{12,... | collective-permute-start | bytes 786440 | tf_op jit(solution)/shard_map/ppermute | solution.py:220
  7.3 10.4 %collective-permute-start = (f32[4,64,256]{2,1,0:T(8,128)}, f32[4,64,256]{2,1,0:T(8,128)S(1)}, u32[]{:S(2)}, u32[]{:S(2)}) collective-permute-start(f32[4,64,256]{2,1,0:T(8,128)} %own_re.1), channel_id=1, source_target_pairs={{0,1},{1,0},{2,3},{3,2},{4,5},{5,4},{6,7},{7,6},{8,9},{9,8},{10,11... | collective-permute-start | bytes 786440 | tf_op jit(solution)/shard_map/ppermute | solution.py:218
  7.4 10.3 %collective-permute-start.1 = (f32[4,64,256]{2,1,0:T(8,128)}, f32[4,64,256]{2,1,0:T(8,128)S(1)}, u32[]{:S(2)}, u32[]{:S(2)}) collective-permute-start(f32[4,64,256]{2,1,0:T(8,128)} %own_im.1), channel_id=1, source_target_pairs={{0,1},{1,0},{2,3},{3,2},{4,5},{5,4},{6,7},{7,6},{8,9},{9,8},{10,11... | collective-permute-start | bytes 786440 | tf_op jit(solution)/shard_map/ppermute | solution.py:218
  11.9 5.8 %collective-permute-start.4 = (f32[4,64,256]{2,1,0:T(8,128)S(1)}, f32[4,64,256]{2,1,0:T(8,128)S(1)}, u32[]{:S(2)}, u32[]{:S(2)}) collective-permute-start(f32[4,64,256]{2,1,0:T(8,128)S(1)} %collective-permute-done.2.far_re), channel_id=1, source_target_pairs={{0,1},{1,0},{2,3},{3,2},{4,5},{5,4},{6,7},{7,6},{8,9},{9,8},{10,11... | collective-permute-start | bytes 786440 | tf_op jit(solution)/shard_map/ppermute | solution.py:221
  16.4 1.5 %collective-permute-start.5 = (f32[4,64,256]{2,1,0:T(8,128)S(1)}, f32[4,64,256]{2,1,0:T(8,128)S(1)}, u32[]{:S(2)}, u32[]{:S(2)}) collective-permute-start(f32[4,64,256]{2,1,0:T(8,128)S(1)} %collective-permute-done.3.far_im), channel_id=1, source_target_pairs={{0,1},{1,0},{2,3},{3,2},{4,5},{5,4},{6,7},{7,6},{8,9},{9,8},{10,11... | collective-permute-start | bytes 786440 | tf_op jit(solution)/shard_map/ppermute | solution.py:221
  17.9 1.6 %copy-start = (bf16[64,128,128]{2,1,0:T(8,128)(2,1)S(1)}, bf16[64,128,128]{2,1,0:T(8,128)(2,1)}, u32[]{:S(2)}) copy-start(bf16[64,128,128]{2,1,0:T(8,128)(2,1)} %measured_ref.1) | copy-start | bytes 6291460
  19.5 0.9 %copy-start.1 = (f32[4,64,256]{2,1,0:T(8,128)S(1)}, f32[4,64,256]{2,1,0:T(8,128)}, u32[]{:S(2)}) copy-start(f32[4,64,256]{2,1,0:T(8,128)} %own_re.1) | copy-start | bytes 786436
  20.5 0.9 %copy-start.2 = (f32[4,64,256]{2,1,0:T(8,128)S(1)}, f32[4,64,256]{2,1,0:T(8,128)}, u32[]{:S(2)}) copy-start(f32[4,64,256]{2,1,0:T(8,128)} %own_im.1) | copy-start | bytes 786436
  21.4 0.9 %copy-start.3 = (f32[2,128,128]{2,1,0:T(8,128)S(1)}, f32[2,128,128]{2,1,0:T(8,128)}, u32[]{:S(2)}) copy-start(f32[2,128,128]{2,1,0:T(8,128)} %probe_ref.1) | copy-start | bytes 393220
  22.3 0.9 %copy-start.4 = (bf16[256,256]{1,0:T(8,128)(2,1)S(1)}, bf16[256,256]{1,0:T(8,128)(2,1)}, u32[]{:S(2)}) copy-start(bf16[256,256]{1,0:T(8,128)(2,1)} %constant.8.clone.dft_right) | copy-start | bytes 393220
  23.2 0.9 %copy-start.5 = (bf16[256,256]{1,0:T(8,128)(2,1)S(1)}, bf16[256,256]{1,0:T(8,128)(2,1)}, u32[]{:S(2)}) copy-start(bf16[256,256]{1,0:T(8,128)(2,1)} %constant.7.clone.dft_left) | copy-start | bytes 393220
  24.1 0.7 copy-start.6
  24.8 0.7 copy-start.7
  45.5 2.0 %collective-permute-start.7 = (f32[2,4,64,256]{3,2,1,0:T(8,128)S(1)}, f32[2,4,64,256]{3,2,1,0:T(8,128)S(1)}, u32[]{:S(2)}, u32[]{:S(2)}) collective-permute-start(f32[2,4,64,256]{3,2,1,0:T(8,128)S(1)} %get-tuple-element.9), channel_id=1, source_target_pairs={{0,1},{1,0},{2,3},{3,2},{4,5},{5,4},{6,7},{7,6},{8,9},{9,8},{10,11... | collective-permute-start | bytes 1572872 | tf_op jit(solution)/shard_map/ppermute | solution.py:251
  45.8 3.6 %collective-permute-start.6 = (f32[2,4,64,256]{3,2,1,0:T(8,128)S(1)}, f32[2,4,64,256]{3,2,1,0:T(8,128)S(1)}, u32[]{:S(2)}, u32[]{:S(2)}) collective-permute-start(f32[2,4,64,256]{3,2,1,0:T(8,128)S(1)} %get-tuple-element.7), channel_id=1, source_target_pairs={{0,1},{1,0},{2,3},{3,2},{4,5},{5,4},{6,7},{7,6},{8,9},{9,8},{10,11... | collective-permute-start | bytes 1572872 | tf_op jit(solution)/shard_map/ppermute | solution.py:251
  47.6 17.8 %collective-permute-start.8 = (f32[2,4,64,256]{3,2,1,0:T(8,128)S(1)}, f32[2,4,64,256]{3,2,1,0:T(8,128)S(1)}, u32[]{:S(2)}, u32[]{:S(2)}) collective-permute-start(f32[2,4,64,256]{3,2,1,0:T(8,128)S(1)} %add.12), channel_id=1, source_target_pairs={{0,2},{1,3},{2,4},{3,5},{4,6},{5,7},{6,8},{7,9},{8,10},{9,11},{10,... | collective-permute-start | bytes 1572872 | tf_op jit(solution)/shard_map/ppermute | solution.py:253

commit v2 on v1

--- a/solution.py
+++ b/solution.py
@@ -11,6 +11,7 @@
 
 AMP_FLOOR = 0.25
 BATCH = 4
+VMEM_BYTES = 60 * 1024 * 1024
 
 
 def dft_tables(patch):
@@ -71,7 +72,7 @@
 
 def compute_kernel(
     taps, rows_ref, cols_ref, live_ref, phase_ref, dft_left, dft_right, probe_ref,
-    own_re, own_im, sib_re, sib_im, far_re, far_im, farsib_re, farsib_im, measured_ref,
+    own_re, own_im, sib_ref, far_ref, farsib_ref, measured_ref,
     keep_ref, give_ref, spill_ref, spillgive_ref,
     window, acc, target, kern_left, kern_right, saved, patches, listed, in_sem, target_sem, out_sem,
 ):
@@ -83,8 +84,16 @@
     pair, parity = member // 2, member % 2
     get_target = pltpu.make_async_copy(measured_ref, target, target_sem)
     get_target.start()
+    has_up = lax.axis_index("tile") * lax.axis_size("pos") + member < lax.axis_size(
+        "tile"
+    ) * lax.axis_size("pos") - 2
     loads = []
-    sources = ((own_re, own_im), (sib_re, sib_im), (far_re, far_im), (farsib_re, farsib_im))
+    sources = (
+        (own_re, own_im),
+        (sib_ref.at[0], sib_ref.at[1]),
+        (far_ref.at[0], far_ref.at[1]),
+        (farsib_ref.at[0], farsib_ref.at[1]),
+    )
     spots = (parity, 1 - parity, 2 + parity, 3 - parity)
     for source, spot in zip(sources, spots):
         for part in range(2):
@@ -96,8 +105,20 @@
                         in_sem.at[len(loads)],
                     )
                 )
-    for load in loads:
+    inner_loads, far_loads = loads[: 4 * parts], loads[4 * parts :]
+    for load in inner_loads:
         load.start()
+
+    @pl.when(has_up)
+    def _():
+        for load in far_loads:
+            load.start()
+
+    @pl.when(jnp.logical_not(has_up))
+    def _():
+        window[:, :, :, 2 * shard :, :] = jnp.zeros(
+            window.shape[:3] + (2 * shard, patch), window.dtype
+        )
 
     def pick(slot, count):
         ok = jnp.logical_and(slot < live_ref[0], rows_ref[slot] // (2 * shard) == pair)
@@ -124,8 +145,14 @@
     kern_re_t, kern_im_t = kern_re.T, kern_im.T
     kern_right[...] = stack_rows(halves([(kern_re_t, -kern_im_t), (kern_im_t, kern_re_t)]))
     acc[...] = jnp.zeros_like(acc)
-    for load in loads:
+    for load in inner_loads:
         load.wait()
+
+    @pl.when(has_up)
+    def _():
+        for load in far_loads:
+            load.wait()
+
     get_target.wait()
 
     def group(step, carry):
@@ -206,29 +233,170 @@
         store.wait()
 
 
+def neighbours():
+    tile, pos = lax.axis_index("tile"), lax.axis_index("pos")
+    members = lax.axis_size("pos")
+    devices = lax.axis_size("tile") * members
+    me = tile * members + pos
+    below, above = (me + devices - 2) % devices, (me + 2) % devices
+    sibling = (tile, pos + 1 - 2 * (pos % 2))
+    lower, upper = (below // members, below % members), (above // members, above % members)
+    return sibling, lower, upper, me >= 2, me < devices - 2
+
+
+def greet(sibling, lower, upper, has_down, has_up):
+    barrier = pltpu.get_barrier_semaphore()
+    mesh_ids = pl.DeviceIdType.MESH
+    pl.semaphore_signal(barrier, inc=1, device_id=sibling, device_id_type=mesh_ids)
+
+    @pl.when(has_down)
+    def _():
+        pl.semaphore_signal(barrier, inc=1, device_id=lower, device_id_type=mesh_ids)
+
+    @pl.when(has_up)
+    def _():
+        pl.semaphore_signal(barrier, inc=1, device_id=upper, device_id_type=mesh_ids)
+
+    pl.semaphore_wait(barrier, 1 + has_down.astype(jnp.int32) + has_up.astype(jnp.int32))
+
+
+def remote(source, target, send, receive, device):
+    return pltpu.make_async_remote_copy(
+        src_ref=source, dst_ref=target, send_sem=send, recv_sem=receive,
+        device_id=device, device_id_type=pl.DeviceIdType.MESH,
+    )
+
+
+def gather_kernel(re_ref, im_ref, sib, far, farsib, far_send, far_recv, fwd_send, fwd_recv, sib_send, sib_recv):
+    sibling, lower, upper, has_down, has_up = neighbours()
+    slices = re_ref.shape[0]
+    fields = (re_ref, im_ref)
+    chunks = [(part, layer) for layer in range(slices) for part in range(2)]
+    outward = [
+        remote(fields[p].at[s], far.at[p, s], far_send.at[k], far_recv.at[k], lower)
+        for k, (p, s) in enumerate(chunks)
+    ]
+    onward = [
+        remote(far.at[p, s], farsib.at[p, s], fwd_send.at[k], fwd_recv.at[k], sibling)
+        for k, (p, s) in enumerate(chunks)
+    ]
+    across = [remote(fields[p], sib.at[p], sib_send.at[p], sib_recv.at[p], sibling) for p in range(2)]
+    greet(sibling, lower, upper, has_down, has_up)
+
+    @pl.when(has_down)
+    def _():
+        for copy in outward:
+            copy.start()
+
+    for copy in across:
+        copy.start()
+
+    @pl.when(has_up)
+    def _():
+        for come, go in zip(outward, onward):
+            come.wait_recv()
+            go.start()
+        for go in onward:
+            go.wait()
+
+    for copy in across:
+        copy.wait()
+
+    @pl.when(has_down)
+    def _():
+        for copy in outward:
+            copy.wait_send()
+
+
+def scatter_kernel(
+    keep, give, spill, spillgive, out_re, out_im,
+    kept, spilled, given, crossed, total, behind,
+    load_sem, keep_sem, cross_send, cross_recv, give_send, give_recv, up_send, up_recv,
+):
+    sibling, lower, upper, has_down, has_up = neighbours()
+    slices = out_re.shape[0]
+    outs = (out_re, out_im)
+    chunks = [(part, layer) for layer in range(slices) for part in range(2)]
+    across = [
+        remote(spillgive.at[p, s], crossed.at[p, s], cross_send.at[k], cross_recv.at[k], sibling)
+        for k, (p, s) in enumerate(chunks)
+    ]
+    gifts = [remote(give.at[p], given.at[p], give_send.at[p], give_recv.at[p], sibling) for p in range(2)]
+    upward = [
+        remote(total.at[p, s], behind.at[p, s], up_send.at[k], up_recv.at[k], upper)
+        for k, (p, s) in enumerate(chunks)
+    ]
+    loads = [
+        pltpu.make_async_copy(spill.at[p, s], spilled.at[p, s], load_sem.at[k])
+        for k, (p, s) in enumerate(chunks)
+    ]
+    load_keep = pltpu.make_async_copy(keep, kept, keep_sem)
+    for load in loads:
+        load.start()
+    greet(sibling, lower, upper, has_down, has_up)
+    for copy in across:
+        copy.start()
+    for copy in gifts:
+        copy.start()
+    load_keep.start()
+    for k, (p, s) in enumerate(chunks):
+        loads[k].wait()
+        across[k].wait_recv()
+        total[p, s] = spilled[p, s] + crossed[p, s]
+
+        @pl.when(has_up)
+        def _():
+            upward[k].start()
+
+    load_keep.wait()
+    for copy in gifts:
+        copy.wait()
+    for p in range(2):
+        outs[p][...] = kept[p] + given[p]
+
+    @pl.when(has_down)
+    def _():
+        for k, (p, s) in enumerate(chunks):
+            upward[k].wait_recv()
+            outs[p][s] = outs[p][s] + behind[p, s]
+
+    for copy in across:
+        copy.wait_send()
+
+    @pl.when(has_up)
+    def _():
+        for copy in upward:
+            copy.wait_send()
+
+
 def local(obj_real, obj_imag, probe, fresnel_phase, row_offset, col_offset, live_count, measured):
     slices, shard, width = obj_real.shape
     patch = probe.shape[-1]
-    members = lax.axis_size("pos")
-    devices = lax.axis_size("tile") * members
     parts = width // patch
     taps = fresnel_phase.shape[0]
-    both = ("tile", "pos")
-    swap = [(d, d ^ 1) for d in range(members)]
-    sib_re, sib_im = lax.ppermute((obj_real, obj_imag), "pos", swap)
-    up = [(d, d - 2) for d in range(2, devices)]
-    far_re, far_im = lax.ppermute((obj_real, obj_imag), both, up)
-    farsib_re, farsib_im = lax.ppermute((far_re, far_im), "pos", swap)
-    phase = jnp.pad(fresnel_phase, (0, patch - taps)).reshape(1, patch)
-    dft_left, dft_right = dft_tables(patch)
+    chunks = 2 * slices
     block = jax.ShapeDtypeStruct((2, slices, shard, width), jnp.float32)
     smem = pl.BlockSpec(memory_space=pltpu.SMEM)
     vmem = pl.BlockSpec(memory_space=pltpu.VMEM)
     anywhere = pl.BlockSpec(memory_space=pl.ANY)
+    dma = pltpu.SemaphoreType.DMA
+    sib, far, farsib = pl.pallas_call(
+        gather_kernel,
+        out_shape=[block] * 3,
+        in_specs=[anywhere] * 2,
+        out_specs=[anywhere] * 3,
+        scratch_shapes=[dma((chunks,))] * 4 + [dma((2,))] * 2,
+        compiler_params=pltpu.CompilerParams(
+            collective_id=0, has_side_effects=True, vmem_limit_bytes=VMEM_BYTES
+        ),
+        name="gather_rows",
+    )(obj_real, obj_imag)
+    phase = jnp.pad(fresnel_phase, (0, patch - taps)).reshape(1, patch)
+    dft_left, dft_right = dft_tables(patch)
     keep, give, spill, spillgive = pl.pallas_call(
         functools.partial(compute_kernel, taps),
         out_shape=[block] * 4,
-        in_specs=[smem] * 3 + [vmem] * 4 + [anywhere] * 9,
+        in_specs=[smem] * 3 + [vmem] * 4 + [anywhere] * 6,
         out_specs=[anywhere] * 4,
         scratch_shapes=[
             pltpu.VMEM((2, slices, parts, 4 * shard, patch), jnp.float32),
@@ -243,16 +411,30 @@
             pltpu.SemaphoreType.DMA,
             pltpu.SemaphoreType.DMA((8 * parts,)),
         ],
-        compiler_params=pltpu.CompilerParams(vmem_limit_bytes=40 * 1024 * 1024),
+        compiler_params=pltpu.CompilerParams(vmem_limit_bytes=VMEM_BYTES),
+        name="patch_gradients",
     )(
         row_offset, col_offset, live_count, phase, dft_left, dft_right, probe,
-        obj_real, obj_imag, sib_re, sib_im, far_re, far_im, farsib_re, farsib_im, measured,
+        obj_real, obj_imag, sib, far, farsib, measured,
     )
-    sib, spillsib = lax.ppermute((give, spillgive), "pos", swap)
-    down = [(d, d + 2) for d in range(devices - 2)]
-    behind = lax.ppermute(spill + spillsib, both, down)
-    total = keep + sib + behind
-    return total[0], total[1]
+    out = jax.ShapeDtypeStruct(obj_real.shape, jnp.float32)
+    return tuple(
+        pl.pallas_call(
+            scatter_kernel,
+            out_shape=[out] * 2,
+            in_specs=[anywhere] * 4,
+            out_specs=[vmem] * 2,
+            scratch_shapes=[pltpu.VMEM(block.shape, jnp.float32)] * 6
+            + [dma((chunks,)), dma]
+            + [dma((chunks,))] * 2
+            + [dma((2,))] * 2
+            + [dma((chunks,))] * 2,
+            compiler_params=pltpu.CompilerParams(
+                collective_id=1, has_side_effects=True, vmem_limit_bytes=VMEM_BYTES
+            ),
+            name="scatter_rows",
+        )(keep, give, spill, spillgive)
+    )
 
 
 def solution(mesh):

time: 66.2 us -> 62.8 us (0.949)
  Pallas kernels: 20 us -> 56.5 us
  waiting for transfers between devices: 26 us -> 0 us
  starting transfers between devices: 9.73 us -> 0 us
  local copies, waits for them, and re-layouts: 9 us -> 4.52 us
    pallas_call x0 -> x2, Pallas kernels: none -> 38.1 us  [the longest x1 21.6 us: local(): pl.pallas_call(scatter_kernel, out_shape=[out] * 2, in_specs=[anywhere] *...]
    ppermute x9 -> x0, waiting for transfers between devices: 26 us -> none  [the longest x1 15.9 us: local(): behind = lax.ppermute(spill + spillsib, both, down)]
    ppermute x9 -> x0, starting transfers between devices: 9.73 us -> none  [the longest x2 6.66 us: local(): far_re, far_im = lax.ppermute((obj_real, obj_imag), both, up)]
    unnamed x16 -> x2, local copies, waits for them, and re-layouts: 7.51 us -> 3.35 us
    pallas_call x1, Pallas kernels: 20 us -> 18.4 us  [local(): pl.pallas_call(functools.partial(compute_kernel, taps), out_shape=[block]...]
    squeeze x1 -> x0, local copies, waits for them, and re-layouts: 0.83 us -> none  [local(): return (total[0], total[1])]
  transfers between devices with their start and end apart: 9 -> 0, of which waited for: 5 -> 0; matrix products, arithmetic and copies ran while one was open for 1% -> 0% of each run, Pallas kernels for 0% -> 0%
where the time goes in v2:
time: 62.8 us; the launch traced here: 62.3 us
  Pallas kernels  56.5 us (90%)
  local copies, waits for them, and re-layouts  4.52 us (7%)
  between operations  1.3 us (2%)
    pallas_call x1, Pallas kernels, local(): pl.pallas_call(scatter_kernel, out_shape=[out] * 2, in_specs=[anywhere] *...  21.6 us
    pallas_call x1, Pallas kernels, local(): pl.pallas_call(functools.partial(compute_kernel, taps), out_shape=[block]...  18.4 us
    pallas_call x1, Pallas kernels, local(): pl.pallas_call(gather_kernel, out_shape=[block] * 3, in_specs=[anywhere]...  16.5 us
    unnamed x2, local copies, waits for them, and re-layouts  3.35 us

profile of v2, /device:TPU:16, one launch (start us, length us, event | category | flops | bytes accessed | tf_op | source)
XLA Modules:
  0.0 62.3 jit_solution(14190312190552601139)
XLA Ops:
  1.3 1.2 %pad_bitcast_fusion.phase_ref = f32[1,128]{1,0:T(1,128)} fusion(f32[33]{0:T(128)} %param.13), kind=kLoop, calls=%fused_computation | loop fusion | bytes 644 | tf_op jit(solution)/shard_map/reshape | solution.py:394
  2.4 16.5 %gather_rows.1 = (f32[2,4,64,256]{3,2,1,0:T(8,128)}, f32[2,4,64,256]{3,2,1,0:T(8,128)}, f32[2,4,64,256]{3,2,1,0:T(8,128)}) custom-call(f32[4,64,256]{2,1,0:T(8,128)} %own_re.1, f32[4,64,256]{2,1,0:T(8,128)} %own_im.1), custom_call_target="tpu_custom_call" | custom-call | tf_op jit(solution)/shard_map/gather_rows/pallas_call | solution.py:383
  18.9 18.4 %patch_gradients.1 = (f32[2,4,64,256]{3,2,1,0:T(8,128)}, f32[2,4,64,256]{3,2,1,0:T(8,128)}, f32[2,4,64,256]{3,2,1,0:T(8,128)}, f32[2,4,64,256]{3,2,1,0:T(8,128)}) custom-call(s32[64]{0:T(128)} %rows_ref.1, s32[64]{0:T(128)} %cols_ref.1, s32[1]{0:T(128)S(6)} %copy.14.live_ref, f32[1,128]{1,0:T(1,128)} %pad_bitcast_fusion.phase_ref, ...), custom_call_target="tpu_custom_call" | custom-call | tf_op jit(solution)/shard_map/patch_gradients/pallas_call | solution.py:396
  37.4 21.6 %scatter_rows.1 = (f32[4,64,256]{2,1,0:T(8,128)}, f32[4,64,256]{2,1,0:T(8,128)}) custom-call(f32[2,4,64,256]{3,2,1,0:T(8,128)} %get-tuple-element.12.keep, f32[2,4,64,256]{3,2,1,0:T(8,128)} %get-tuple-element.13.give, f32[2,4,64,256]{3,2,1,0:T(8,128)} %get-tuple-element.14.spill, f32[2,4,64,256]{3,2,1,0:T(8,128)} %get-tuple-element.15.spillgive), custom_call_target="tpu_custom_call" | custom-call | tf_op jit(solution)/shard_map/scatter_rows/pallas_call | solution.py:422
  58.9 1.7 %copy.15 = f32[4,64,256]{2,1,0:T(8,128)} copy(f32[4,64,256]{2,1,0:T(8,128)} %get-tuple-element.18) | data formatting | bytes 524288
  60.6 1.7 %copy.16 = f32[4,64,256]{2,1,0:T(8,128)} copy(f32[4,64,256]{2,1,0:T(8,128)} %get-tuple-element.19) | data formatting | bytes 524288

commit v3 on v1

v3 whole, which is shorter than its diff:
```python
import functools

import jax
import jax.numpy as jnp
import ml_dtypes
import numpy as np
from jax import lax
from jax.experimental import pallas as pl
from jax.experimental.pallas import tpu as pltpu
from jax.sharding import PartitionSpec as P

AMP_FLOOR = 0.25
BATCH = 4
CHAIN = 2
VMEM_BYTES = 60 * 1024 * 1024


def dft_tables(patch):
    grid = np.arange(patch)
    product = (grid[:, None] * grid[None, :] % patch).astype(np.float32)
    angle = np.float32(2.0 * np.pi / patch) * product
    norm = np.float32(1.0) / np.sqrt(np.float32(patch))
    real = (np.cos(angle) * norm).astype(ml_dtypes.bfloat16)
    imag = (-np.sin(angle) * norm).astype(ml_dtypes.bfloat16)
    left = np.block([[real, -imag], [imag, real]])
    right = np.block([[real.T, imag.T], [-imag.T, real.T]])
    return jnp.asarray(left), jnp.asarray(right)


def dot(left, right):
    return jnp.dot(left, right, preferred_element_type=jnp.float32)


def stack_rows(pairs):
    return jnp.concatenate([jnp.concatenate(pair, axis=0) for pair in pairs], axis=1)


def stack_cols(pairs):
    return jnp.concatenate([jnp.concatenate(pair, axis=1) for pair in pairs], axis=0)


def split_rows(array, patch):
    count = array.shape[1] // patch
    return [
        (array[:patch, b * patch : (b + 1) * patch], array[patch:, b * patch : (b + 1) * patch])
        for b in range(count)
    ]


def split_cols(array, patch):
    count = array.shape[0] // patch
    return [
        (array[b * patch : (b + 1) * patch, :patch], array[b * patch : (b + 1) * patch, patch:])
        for b in range(count)
    ]


def halves(pairs):
    return [(a.astype(jnp.bfloat16), b.astype(jnp.bfloat16)) for a, b in pairs]


def forward_two_sided(left, right, pairs):
    patch = pairs[0][0].shape[0]
    inner = split_rows(dot(left, stack_rows(halves(pairs))), patch)
    return split_cols(dot(stack_cols(halves(inner)), right), patch)


def backward_two_sided(left, right, pairs):
    patch = pairs[0][0].shape[0]
    inner = split_cols(dot(stack_cols(halves(pairs)), left), patch)
    return split_rows(dot(right, stack_rows(halves(inner))), patch)


def compute_kernel(
    taps, rows_ref, cols_ref, live_ref, phase_ref, dft_left, dft_right, probe_ref,
    own_re, own_im, near_ref, nearsib_ref, far_ref, farsib_ref, measured_ref,
    near_keep, near_give, far_keep, far_give,
    window, acc, target, kern_left, kern_right, saved, patches, listed, in_sem, target_sem, out_sem,
):
    slices, shard, width = own_re.shape
    patch = probe_ref.shape[-1]
    slots = rows_ref.shape[0]
    parts = width // patch
    member = lax.axis_index("pos")
    parity = member % 2
    get_target = pltpu.make_async_copy(measured_ref, target, target_sem)
    get_target.start()
    outer = member < 2
    ahead = jnp.logical_and(outer, lax.axis_index("tile") + 1 < lax.axis_size("tile"))
    base = jnp.where(outer, 2 * shard, 0)
    spots = (parity, 1 - parity, 2 + parity, 3 - parity)

    def loads_of(real, imag, place):
        return [
            pltpu.make_async_copy(
                source.at[:, :, pl.ds(half * patch, patch)],
                window.at[part, :, half, pl.ds(spots[place] * shard, shard), :],
                in_sem.at[(place * 2 + part) * parts + half],
            )
            for part, source in enumerate((real, imag))
            for half in range(parts)
        ]

    near_loads = loads_of(near_ref.at[0], near_ref.at[1], 0)
    near_loads += loads_of(nearsib_ref.at[0], nearsib_ref.at[1], 1)
    own_loads = loads_of(own_re, own_im, 2)
    far_loads = loads_of(far_ref.at[0], far_ref.at[1], 2)
    farsib_loads = loads_of(farsib_ref.at[0], farsib_ref.at[1], 3)
    for load in near_loads:
        load.start()

    @pl.when(jnp.logical_not(outer))
    def _():
        for load in own_loads + farsib_loads:
            load.start()

    @pl.when(ahead)
    def _():
        for load in far_loads + farsib_loads:
            load.start()

    @pl.when(jnp.logical_and(outer, jnp.logical_not(ahead)))
    def _():
        window[:, :, :, 2 * shard :, :] = jnp.zeros(
            window.shape[:3] + (2 * shard, patch), window.dtype
        )

    def pick(slot, count):
        ok = jnp.logical_and(slot < live_ref[0], (rows_ref[slot] >= 2 * shard) == outer)
        take = jnp.logical_and(ok, count % 2 == parity)
        listed[jnp.where(take, count // 2, slots)] = slot
        return count + ok.astype(jnp.int32)

    total = lax.fori_loop(0, slots, pick, jnp.int32(0))
    mine = (total + 1 - parity) // 2

    row = lax.broadcasted_iota(jnp.int32, (patch, patch), 0)
    col = lax.broadcasted_iota(jnp.int32, (patch, patch), 1)
    band = jnp.logical_and(col - row + taps // 2 >= 0, col - row + taps // 2 < taps)
    scale = 1.0 / jnp.sqrt(jnp.float32(taps))

    def toeplitz(values):
        wide = jnp.broadcast_to(values, (patch, patch))
        moved = pltpu.roll(wide, patch - taps // 2, 1, stride=1, stride_axis=0)
        return jnp.where(band, moved, 0.0)

    kern_re = toeplitz(jnp.cos(phase_ref[...]) * scale)
    kern_im = toeplitz(jnp.sin(phase_ref[...]) * scale)
    kern_left[...] = stack_rows(halves([(kern_re, kern_im), (-kern_im, kern_re)]))
    kern_re_t, kern_im_t = kern_re.T, kern_im.T
    kern_right[...] = stack_rows(halves([(kern_re_t, -kern_im_t), (kern_im_t, kern_re_t)]))
    acc[...] = jnp.zeros_like(acc)
    for load in near_loads:
        load.wait()

    @pl.when(jnp.logical_or(jnp.logical_not(outer), ahead))
    def _():
        for load in far_loads + farsib_loads:
            load.wait()

    get_target.wait()

    def group(first, size):
        every = range(size)
        chains = [list(every)[c : c + CHAIN] for c in range(0, size, CHAIN)]
        index = [listed[jnp.minimum(first + b, mine - 1)] for b in every]
        weight = [(first + b < mine).astype(jnp.float32) for b in every]
        top = [rows_ref[i] - base for i in index]
        left = [cols_ref[i] for i in index]
        back = [(patch - x) % patch for x in left]
        forth = [x % patch for x in left]
        inside = [col >= x for x in left]

        def cut(layer, b, part):
            a0 = window[part, layer, 0, pl.ds(top[b], patch), :]
            a1 = window[part, layer, 1, pl.ds(top[b], patch), :]
            return pltpu.roll(jnp.where(inside[b], a0, a1), back[b], 1)

        waves = [(probe_ref[0], probe_ref[1]) for _ in every]
        for layer in range(slices):
            for chain in chains:
                nxt = []
                for b in chain:
                    o_re, o_im = cut(layer, b, 0), cut(layer, b, 1)
                    w_re, w_im = waves[b]
                    if layer:
                        patches[layer - 1, b, 0] = o_re
                        patches[layer - 1, b, 1] = o_im
                        saved[layer - 1, b, 0] = w_re
                        saved[layer - 1, b, 1] = w_im
                    nxt.append((w_re * o_re - w_im * o_im, w_re * o_im + w_im * o_re))
                last = layer + 1 == slices
                lhs, rhs = (dft_left, dft_right) if last else (kern_left, kern_right)
                for b, wave in zip(chain, forward_two_sided(lhs[...], rhs[...], nxt)):
                    waves[b] = wave
        grads = list(waves)
        for chain in chains:
            nxt = []
            for b in chain:
                f_re, f_im = waves[b]
                amplitude = jnp.sqrt(f_re * f_re + f_im * f_im + AMP_FLOOR)
                t = target[index[b]].astype(jnp.float32)
                ratio = weight[b] * (amplitude - t) / amplitude
                nxt.append((f_re * ratio, f_im * ratio))
            for b, grad in zip(chain, backward_two_sided(dft_left[...], dft_right[...], nxt)):
                grads[b] = grad
        for layer in reversed(range(slices)):
            for chain in chains:
                nxt = []
                for b in chain:
                    g_re, g_im = grads[b]
                    if layer:
                        w_re, w_im = saved[layer - 1, b, 0], saved[layer - 1, b, 1]
                        o_re, o_im = patches[layer - 1, b, 0], patches[layer - 1, b, 1]
                        nxt.append((o_re * g_re + o_im * g_im, o_re * g_im - o_im * g_re))
                    else:
                        w_re, w_im = probe_ref[0], probe_ref[1]
                    terms = (w_re * g_re + w_im * g_im, w_re * g_im - w_im * g_re)
                    for part in range(2):
                        moved = pltpu.roll(terms[part], forth[b], 1)
                        spot = pl.ds(top[b], patch)
                        acc[part, layer, 0, spot, :] += jnp.where(inside[b], moved, 0.0)
                        acc[part, layer, 1, spot, :] += jnp.where(inside[b], 0.0, moved)
                if layer:
                    for b, grad in zip(chain, backward_two_sided(kern_left[...], kern_right[...], nxt)):
                        grads[b] = grad

    rounds = (mine + BATCH // 2 - 1) // BATCH

    def full(step, carry):
        group(step * BATCH, BATCH)
        return carry

    lax.fori_loop(0, rounds, full, 0)

    @pl.when(rounds * BATCH < mine)
    def _():
        group(rounds * BATCH, BATCH // 2)

    stores = []
    for result, spot in zip((near_keep, near_give, far_keep, far_give), spots):
        for part in range(2):
            for half in range(parts):
                stores.append(
                    pltpu.make_async_copy(
                        acc.at[part, :, half, pl.ds(spot * shard, shard), :],
                        result.at[part, :, :, pl.ds(half * patch, patch)],
                        out_sem.at[len(stores)],
                    )
                )
    for store in stores:
        store.start()
    for store in stores:
        store.wait()


def neighbours():
    tile, pos = lax.axis_index("tile"), lax.axis_index("pos")
    tiles = lax.axis_size("tile")
    sibling = (tile, pos + 1 - 2 * (pos % 2))
    across = (tile, (pos + 2) % 4)
    lower, upper = ((tile + tiles - 1) % tiles, pos), ((tile + 1) % tiles, pos)
    outer = pos < 2
    has_down = jnp.logical_and(outer, tile > 0)
    has_up = jnp.logical_and(outer, tile < tiles - 1)
    return sibling, across, lower, upper, outer, has_down, has_up


def greet(sibling, across, lower, upper, has_down, has_up):
    barrier = pltpu.get_barrier_semaphore()
    mesh_ids = pl.DeviceIdType.MESH
    pl.semaphore_signal(barrier, inc=1, device_id=sibling, device_id_type=mesh_ids)
    pl.semaphore_signal(barrier, inc=1, device_id=across, device_id_type=mesh_ids)

    @pl.when(has_down)
    def _():
        pl.semaphore_signal(barrier, inc=1, device_id=lower, device_id_type=mesh_ids)

    @pl.when(has_up)
    def _():
        pl.semaphore_signal(barrier, inc=1, device_id=upper, device_id_type=mesh_ids)

    pl.semaphore_wait(barrier, 2 + has_down.astype(jnp.int32) + has_up.astype(jnp.int32))


def remote(source, target, send, receive, device):
    return pltpu.make_async_remote_copy(
        src_ref=source, dst_ref=target, send_sem=send, recv_sem=receive,
        device_id=device, device_id_type=pl.DeviceIdType.MESH,
    )


def gather_kernel(
    re_ref, im_ref, near, nearsib, far, farsib,
    near_send, near_recv, far_send, far_recv, pass_send, pass_recv, fpass_send, fpass_recv,
):
    sibling, across, lower, upper, outer, has_down, has_up = neighbours()
    slices = re_ref.shape[0]
    fields = (re_ref, im_ref)
    chunks = list(enumerate((part, layer) for layer in range(slices) for part in range(2)))
    over = [remote(fields[p].at[s], near.at[p, s], near_send.at[k], near_recv.at[k], across) for k, (p, s) in chunks]
    down = [remote(fields[p].at[s], far.at[p, s], far_send.at[k], far_recv.at[k], lower) for k, (p, s) in chunks]
    over_pass = [remote(near.at[p, s], nearsib.at[p, s], pass_send.at[k], pass_recv.at[k], sibling) for k, (p, s) in chunks]
    down_pass = [remote(far.at[p, s], farsib.at[p, s], fpass_send.at[k], fpass_recv.at[k], sibling) for k, (p, s) in chunks]
    own_pass = [remote(fields[p].at[s], farsib.at[p, s], fpass_send.at[k], fpass_recv.at[k], sibling) for k, (p, s) in chunks]
    greet(sibling, across, lower, upper, has_down, has_up)

    @pl.when(has_down)
    def _():
        for one, other in zip(over, down):
            other.start()
            one.start()

    @pl.when(jnp.logical_not(has_down))
    def _():
        for one in over:
            one.start()

    @pl.when(jnp.logical_not(outer))
    def _():
        for copy in own_pass:
            copy.start()

    for k, _ in chunks:
        over[k].wait_recv()
        over_pass[k].start()

        @pl.when(has_up)
        def _():
            down[k].wait_recv()
            down_pass[k].start()

    @pl.when(has_up)
    def _():
        for copy in down_pass:
            copy.wait()

    @pl.when(jnp.logical_not(outer))
    def _():
        for copy in own_pass:
            copy.wait()

    for k, _ in chunks:
        over_pass[k].wait()
        over[k].wait_send()

    @pl.when(has_down)
    def _():
        for copy in down:
            copy.wait_send()


def scatter_kernel(
    near_keep, near_give, far_keep, far_give, from_near, from_far,
    near_kept, near_got, near_sum, far_kept, far_got, far_sum,
    nk_sem, fk_sem, ng_send, ng_recv, fg_send, fg_recv, near_send, near_recv, far_send, far_recv,
):
    sibling, across, lower, upper, outer, has_down, has_up = neighbours()
    slices = near_keep.shape[1]
    chunks = list(enumerate((part, layer) for layer in range(slices) for part in range(2)))
    near_loads = [pltpu.make_async_copy(near_keep.at[p, s], near_kept.at[p, s], nk_sem.at[k]) for k, (p, s) in chunks]
    far_loads = [pltpu.make_async_copy(far_keep.at[p, s], far_kept.at[p, s], fk_sem.at[k]) for k, (p, s) in chunks]
    near_gifts = [remote(near_give.at[p, s], near_got.at[p, s], ng_send.at[k], ng_recv.at[k], sibling) for k, (p, s) in chunks]
    far_gifts = [remote(far_give.at[p, s], far_got.at[p, s], fg_send.at[k], fg_recv.at[k], sibling) for k, (p, s) in chunks]
    over = [remote(near_sum.at[p, s], from_near.at[p, s], near_send.at[k], near_recv.at[k], across) for k, (p, s) in chunks]
    up = [remote(far_sum.at[p, s], from_far.at[p, s], far_send.at[k], far_recv.at[k], upper) for k, (p, s) in chunks]
    hold = [pltpu.make_async_copy(far_sum.at[p, s], from_far.at[p, s], far_send.at[k]) for k, (p, s) in chunks]
    for k, _ in chunks:
        near_loads[k].start()
        far_loads[k].start()
    greet(sibling, across, lower, upper, has_down, has_up)
    for k, _ in chunks:
        near_gifts[k].start()
        far_gifts[k].start()
    for k, (p, s) in chunks:
        near_loads[k].wait()
        near_gifts[k].wait_recv()
        near_sum[p, s] = near_kept[p, s] + near_got[p, s]
        over[k].start()
        far_loads[k].wait()
        far_gifts[k].wait_recv()
        far_sum[p, s] = far_kept[p, s] + far_got[p, s]

        @pl.when(has_up)
        def _():
            up[k].start()

        @pl.when(jnp.logical_not(outer))
        def _():
            hold[k].start()

    for k, _ in chunks:
        near_gifts[k].wait_send()
        far_gifts[k].wait_send()
        over[k].wait()

    @pl.when(jnp.logical_not(outer))
    def _():
        for copy in hold:
            copy.wait()

    @pl.when(has_up)
    def _():
        for copy in up:
            copy.wait_send()

    @pl.when(has_down)
    def _():
        for copy in up:
            copy.wait_recv()


def local(obj_real, obj_imag, probe, fresnel_phase, row_offset, col_offset, live_count, measured):
    slices, shard, width = obj_real.shape
    patch = probe.shape[-1]
    parts = width // patch
    taps = fresnel_phase.shape[0]
    chunks = 2 * slices
    assert lax.axis_size("pos") == 4 and 2 * shard == patch and parts == 2
    block = jax.ShapeDtypeStruct((2, slices, shard, width), jnp.float32)
    smem = pl.BlockSpec(memory_space=pltpu.SMEM)
    vmem = pl.BlockSpec(memory_space=pltpu.VMEM)
    anywhere = pl.BlockSpec(memory_space=pl.ANY)
    dma = pltpu.SemaphoreType.DMA
    near, nearsib, far, farsib = pl.pallas_call(
        gather_kernel,
        out_shape=[block] * 4,
        in_specs=[anywhere] * 2,
        out_specs=[anywhere] * 4,
        scratch_shapes=[dma((chunks,))] * 8,
        compiler_params=pltpu.CompilerParams(
            collective_id=0, has_side_effects=True, vmem_limit_bytes=VMEM_BYTES
        ),
        name="gather_rows",
    )(obj_real, obj_imag)
    phase = jnp.pad(fresnel_phase, (0, patch - taps)).reshape(1, patch)
    dft_left, dft_right = dft_tables(patch)
    parts_of_sum = pl.pallas_call(
        functools.partial(compute_kernel, taps),
        out_shape=[block] * 4,
        in_specs=[smem] * 3 + [vmem] * 4 + [anywhere] * 7,
        out_specs=[anywhere] * 4,
        scratch_shapes=[
            pltpu.VMEM((2, slices, parts, 4 * shard, patch), jnp.float32),
            pltpu.VMEM((2, slices, parts, 4 * shard, patch), jnp.float32),
            pltpu.VMEM(measured.shape, measured.dtype),
            pltpu.VMEM((2 * patch, 2 * patch), jnp.bfloat16),
            pltpu.VMEM((2 * patch, 2 * patch), jnp.bfloat16),
            pltpu.VMEM((slices - 1, BATCH, 2, patch, patch), jnp.float32),
            pltpu.VMEM((slices - 1, BATCH, 2, patch, patch), jnp.float32),
            pltpu.SMEM((row_offset.shape[0] + 8,), jnp.int32),
            pltpu.SemaphoreType.DMA((8 * parts,)),
            pltpu.SemaphoreType.DMA,
            pltpu.SemaphoreType.DMA((8 * parts,)),
        ],
        compiler_params=pltpu.CompilerParams(vmem_limit_bytes=VMEM_BYTES),
        name="patch_gradients",
    )(
        row_offset, col_offset, live_count, phase, dft_left, dft_right, probe,
        obj_real, obj_imag, near, nearsib, far, farsib, measured,
    )
    from_near, from_far = pl.pallas_call(
        scatter_kernel,
        out_shape=[block] * 2,
        in_specs=[anywhere] * 4,
        out_specs=[anywhere] * 2,
        scratch_shapes=[pltpu.VMEM(block.shape, jnp.float32)] * 6 + [dma((chunks,))] * 10,
        compiler_params=pltpu.CompilerParams(
            collective_id=1, has_side_effects=True, vmem_limit_bytes=VMEM_BYTES
        ),
        name="scatter_rows",
    )(*parts_of_sum)
    alone = jnp.logical_and(lax.axis_index("tile") == 0, lax.axis_index("pos") < 2)
    return tuple(from_near[p] + jnp.where(alone, 0.0, from_far[p]) for p in range(2))


def solution(mesh):
    in_specs = (
        P(None, ("tile", "pos"), None),
        P(None, ("tile", "pos"), None),
        P(),
        P(),
        P("tile"),
        P("tile"),
        P("tile"),
        P("tile", None, None),
    )
    out_specs = (P(None, ("tile", "pos"), None), P(None, ("tile", "pos"), None))
    return jax.shard_map(local, mesh=mesh, in_specs=in_specs, out_specs=out_specs, check_vma=False)
```

time: 66.2 us -> 60.1 us (0.908)
  the two profiles are of different devices: /device:TPU:16 before, /device:TPU:25 now
where the time goes in v3:
time: 60.1 us; the launch traced here: 59.8 us
  Pallas kernels  55.3 us (92%)
  other arithmetic  2.05 us (3%)
  between operations  1.31 us (2%)
  local copies, waits for them, and re-layouts  1.17 us (2%)
    pallas_call x1, Pallas kernels, local(): pl.pallas_call(scatter_kernel, out_shape=[block] * 2, in_specs=[anywhere]...  22.8 us
    pallas_call x1, Pallas kernels, local(): pl.pallas_call(gather_kernel, out_shape=[block] * 4, in_specs=[anywhere]...  17.4 us
    pallas_call x1, Pallas kernels, local(): pl.pallas_call(functools.partial(compute_kernel, taps), out_shape=[block]...  15.1 us
    add x1, other arithmetic, local(): from_near[p] + jnp.where(alone, 0.0, from_far[p])  2.05 us

profile of v3, /device:TPU:25, one launch (start us, length us, event | category | flops | bytes accessed | tf_op | source)
XLA Modules:
  0.0 59.8 jit_solution(9623944478238125080)
XLA Ops:
  0.6 17.4 %gather_rows.1 = (f32[2,4,64,256]{3,2,1,0:T(8,128)}, f32[2,4,64,256]{3,2,1,0:T(8,128)}, f32[2,4,64,256]{3,2,1,0:T(8,128)}, f32[2,4,64,256]{3,2,1,0:T(8,128)}) custom-call(f32[4,64,256]{2,1,0:T(8,128)} %own_re.1, f32[4,64,256]{2,1,0:T(8,128)} %own_im.1), custom_call_target="tpu_custom_call" | custom-call | tf_op jit(solution)/shard_map/gather_rows/pallas_call | solution.py:425
  18.7 1.2 %pad_bitcast_fusion.phase_ref = f32[1,128]{1,0:T(1,128)} fusion(f32[33]{0:T(128)} %param.13), kind=kLoop, calls=%fused_computation.2 | loop fusion | bytes 644 | tf_op jit(solution)/shard_map/reshape | solution.py:436
  19.9 15.1 %patch_gradients.1 = (f32[2,4,64,256]{3,2,1,0:T(8,128)}, f32[2,4,64,256]{3,2,1,0:T(8,128)}, f32[2,4,64,256]{3,2,1,0:T(8,128)}, f32[2,4,64,256]{3,2,1,0:T(8,128)}) custom-call(s32[64]{0:T(128)} %rows_ref.1, s32[64]{0:T(128)} %cols_ref.1, s32[1]{0:T(128)S(6)} %copy.12.live_ref, f32[1,128]{1,0:T(1,128)} %pad_bitcast_fusion.phase_ref, ...), custom_call_target="tpu_custom_call" | custom-call | tf_op jit(solution)/shard_map/patch_gradients/pallas_call | solution.py:438
  35.0 22.8 %scatter_rows.1 = (f32[2,4,64,256]{3,2,1,0:T(8,128)}, f32[2,4,64,256]{3,2,1,0:T(8,128)}) custom-call(f32[2,4,64,256]{3,2,1,0:T(8,128)} %get-tuple-element.16.near_keep, f32[2,4,64,256]{3,2,1,0:T(8,128)} %get-tuple-element.17.near_give, f32[2,4,64,256]{3,2,1,0:T(8,128)} %get-tuple-element.18.far_keep, f32[2,4,64,256]{3,2,1,0:T(8,128)} %get-tuple-element.19.far_give), custom_call_target="tpu_custom_call" | custom-call | tf_op jit(solution)/shard_map/scatter_rows/pallas_call | solution.py:462
  57.8 2.0 %add_bitcast_fusion = (f32[4,64,256]{2,1,0:T(8,128)}, f32[4,64,256]{2,1,0:T(8,128)}) fusion(f32[2,4,64,256]{3,2,1,0:T(8,128)} %get-tuple-element.21, f32[2,4,64,256]{3,2,1,0:T(8,128)} %get-tuple-element.20, pred[]{:T(512)S(6)} %and.5), kind=kLoop, calls=%fused_computation | loop fusion | flops 262144 | bytes 1572865 | tf_op jit(solution)/shard_map/add | solution.py:474

commit v4 on v3

--- a/solution.py
+++ b/solution.py
@@ -73,9 +73,9 @@
 
 def compute_kernel(
     taps, rows_ref, cols_ref, live_ref, phase_ref, dft_left, dft_right, probe_ref,
-    own_re, own_im, near_ref, nearsib_ref, far_ref, farsib_ref, measured_ref,
-    near_keep, near_give, far_keep, far_give,
-    window, acc, target, kern_left, kern_right, saved, patches, listed, in_sem, target_sem, out_sem,
+    own_re, own_im, sib_ref, near_ref, nearsib_ref, far_ref, farsib_ref, measured_ref,
+    own_keep, own_give, near_keep, near_give, far_keep, far_give,
+    window, acc, target, kern_left, kern_right, saved, patches, phases, in_sem, target_sem, out_sem,
 ):
     slices, shard, width = own_re.shape
     patch = probe_ref.shape[-1]
@@ -85,10 +85,10 @@
     parity = member % 2
     get_target = pltpu.make_async_copy(measured_ref, target, target_sem)
     get_target.start()
-    outer = member < 2
-    ahead = jnp.logical_and(outer, lax.axis_index("tile") + 1 < lax.axis_size("tile"))
-    base = jnp.where(outer, 2 * shard, 0)
-    spots = (parity, 1 - parity, 2 + parity, 3 - parity)
+    pair = member // 2
+    ahead = lax.axis_index("tile") + 1 < lax.axis_size("tile")
+    rank = (pair * 2 + parity, pair * 2 + 1 - parity)
+    spots = (rank[0], rank[1], 2 - pair * 2 + parity, 3 - pair * 2 - parity, 4 + parity, 5 - parity)
 
     def loads_of(real, imag, place):
         return [
@@ -101,38 +101,27 @@
             for half in range(parts)
         ]
 
-    near_loads = loads_of(near_ref.at[0], near_ref.at[1], 0)
-    near_loads += loads_of(nearsib_ref.at[0], nearsib_ref.at[1], 1)
-    own_loads = loads_of(own_re, own_im, 2)
-    far_loads = loads_of(far_ref.at[0], far_ref.at[1], 2)
-    farsib_loads = loads_of(farsib_ref.at[0], farsib_ref.at[1], 3)
+    near_loads = loads_of(own_re, own_im, 0)
+    for place, block in enumerate((sib_ref, near_ref, nearsib_ref)):
+        near_loads += loads_of(block.at[0], block.at[1], place + 1)
+    far_loads = loads_of(far_ref.at[0], far_ref.at[1], 4)
+    far_loads += loads_of(farsib_ref.at[0], farsib_ref.at[1], 5)
     for load in near_loads:
         load.start()
 
-    @pl.when(jnp.logical_not(outer))
-    def _():
-        for load in own_loads + farsib_loads:
+    @pl.when(ahead)
+    def _():
+        for load in far_loads:
             load.start()
 
-    @pl.when(ahead)
-    def _():
-        for load in far_loads + farsib_loads:
-            load.start()
-
-    @pl.when(jnp.logical_and(outer, jnp.logical_not(ahead)))
-    def _():
-        window[:, :, :, 2 * shard :, :] = jnp.zeros(
+    @pl.when(jnp.logical_not(ahead))
+    def _():
+        window[:, :, :, 4 * shard :, :] = jnp.zeros(
             window.shape[:3] + (2 * shard, patch), window.dtype
         )
 
-    def pick(slot, count):
-        ok = jnp.logical_and(slot < live_ref[0], (rows_ref[slot] >= 2 * shard) == outer)
-        take = jnp.logical_and(ok, count % 2 == parity)
-        listed[jnp.where(take, count // 2, slots)] = slot
-        return count + ok.astype(jnp.int32)
-
-    total = lax.fori_loop(0, slots, pick, jnp.int32(0))
-    mine = (total + 1 - parity) // 2
+    members = lax.axis_size("pos")
+    mine = jnp.maximum(live_ref[0] - member + members - 1, 0) // members
 
     row = lax.broadcasted_iota(jnp.int32, (patch, patch), 0)
     col = lax.broadcasted_iota(jnp.int32, (patch, patch), 1)
@@ -144,8 +133,10 @@
         moved = pltpu.roll(wide, patch - taps // 2, 1, stride=1, stride_axis=0)
         return jnp.where(band, moved, 0.0)
 
-    kern_re = toeplitz(jnp.cos(phase_ref[...]) * scale)
-    kern_im = toeplitz(jnp.sin(phase_ref[...]) * scale)
+    phases[...] = jnp.zeros_like(phases)
+    phases[:, :taps] = phase_ref[...]
+    kern_re = toeplitz(jnp.cos(phases[...]) * scale)
+    kern_im = toeplitz(jnp.sin(phases[...]) * scale)
     kern_left[...] = stack_rows(halves([(kern_re, kern_im), (-kern_im, kern_re)]))
     kern_re_t, kern_im_t = kern_re.T, kern_im.T
     kern_right[...] = stack_rows(halves([(kern_re_t, -kern_im_t), (kern_im_t, kern_re_t)]))
@@ -153,9 +144,9 @@
     for load in near_loads:
         load.wait()
 
-    @pl.when(jnp.logical_or(jnp.logical_not(outer), ahead))
-    def _():
-        for load in far_loads + farsib_loads:
+    @pl.when(ahead)
+    def _():
+        for load in far_loads:
             load.wait()
 
     get_target.wait()
@@ -163,9 +154,9 @@
     def group(first, size):
         every = range(size)
         chains = [list(every)[c : c + CHAIN] for c in range(0, size, CHAIN)]
-        index = [listed[jnp.minimum(first + b, mine - 1)] for b in every]
+        index = [member + members * jnp.minimum(first + b, mine - 1) for b in every]
         weight = [(first + b < mine).astype(jnp.float32) for b in every]
-        top = [rows_ref[i] - base for i in index]
+        top = [rows_ref[i] for i in index]
         left = [cols_ref[i] for i in index]
         back = [(patch - x) % patch for x in left]
         forth = [x % patch for x in left]
@@ -225,20 +216,14 @@
                     for b, grad in zip(chain, backward_two_sided(kern_left[...], kern_right[...], nxt)):
                         grads[b] = grad
 
-    rounds = (mine + BATCH // 2 - 1) // BATCH
-
     def full(step, carry):
         group(step * BATCH, BATCH)
         return carry
 
-    lax.fori_loop(0, rounds, full, 0)
-
-    @pl.when(rounds * BATCH < mine)
-    def _():
-        group(rounds * BATCH, BATCH // 2)
+    lax.fori_loop(0, (mine + BATCH - 1) // BATCH, full, 0)
 
     stores = []
-    for result, spot in zip((near_keep, near_give, far_keep, far_give), spots):
+    for result, spot in zip((own_keep, own_give, near_keep, near_give, far_keep, far_give), spots):
         for part in range(2):
             for half in range(parts):
                 stores.append(
@@ -260,10 +245,7 @@
     sibling = (tile, pos + 1 - 2 * (pos % 2))
     across = (tile, (pos + 2) % 4)
     lower, upper = ((tile + tiles - 1) % tiles, pos), ((tile + 1) % tiles, pos)
-    outer = pos < 2
-    has_down = jnp.logical_and(outer, tile > 0)
-    has_up = jnp.logical_and(outer, tile < tiles - 1)
-    return sibling, across, lower, upper, outer, has_down, has_up
+    return sibling, across, lower, upper, pos < 2, tile > 0, tile < tiles - 1
 
 
 def greet(sibling, across, lower, upper, has_down, has_up):
@@ -291,8 +273,8 @@
 
 
 def gather_kernel(
-    re_ref, im_ref, near, nearsib, far, farsib,
-    near_send, near_recv, far_send, far_recv, pass_send, pass_recv, fpass_send, fpass_recv,
+    re_ref, im_ref, sib, near, nearsib, far, farsib,
+    sib_send, sib_recv, near_send, near_recv, far_send, far_recv, pass_send, pass_recv, fpass_send, fpass_recv,
 ):
     sibling, across, lower, upper, outer, has_down, has_up = neighbours()
     slices = re_ref.shape[0]
@@ -300,46 +282,44 @@
     chunks = list(enumerate((part, layer) for layer in range(slices) for part in range(2)))
     over = [remote(fields[p].at[s], near.at[p, s], near_send.at[k], near_recv.at[k], across) for k, (p, s) in chunks]
     down = [remote(fields[p].at[s], far.at[p, s], far_send.at[k], far_recv.at[k], lower) for k, (p, s) in chunks]
+    relay = [remote(near.at[p, s], far.at[p, s], far_send.at[k], far_recv.at[k], lower) for k, (p, s) in chunks]
     over_pass = [remote(near.at[p, s], nearsib.at[p, s], pass_send.at[k], pass_recv.at[k], sibling) for k, (p, s) in chunks]
     down_pass = [remote(far.at[p, s], farsib.at[p, s], fpass_send.at[k], fpass_recv.at[k], sibling) for k, (p, s) in chunks]
-    own_pass = [remote(fields[p].at[s], farsib.at[p, s], fpass_send.at[k], fpass_recv.at[k], sibling) for k, (p, s) in chunks]
+    own_pass = [remote(fields[p], sib.at[p], sib_send.at[p], sib_recv.at[p], sibling) for p in range(2)]
     greet(sibling, across, lower, upper, has_down, has_up)
-
-    @pl.when(has_down)
-    def _():
-        for one, other in zip(over, down):
+    direct = jnp.logical_and(has_down, outer)
+    relayed = jnp.logical_and(has_down, jnp.logical_not(outer))
+
+    for one in over:
+        one.start()
+
+    @pl.when(direct)
+    def _():
+        for other in down:
             other.start()
-            one.start()
-
-    @pl.when(jnp.logical_not(has_down))
-    def _():
-        for one in over:
-            one.start()
-
-    @pl.when(jnp.logical_not(outer))
-    def _():
-        for copy in own_pass:
-            copy.start()
+
+    for copy in own_pass:
+        copy.start()
 
     for k, _ in chunks:
         over[k].wait_recv()
+
+        @pl.when(relayed)
+        def _():
+            relay[k].start()
+
         over_pass[k].start()
 
-        @pl.when(has_up)
-        def _():
+    @pl.when(has_up)
+    def _():
+        for k, _ in chunks:
             down[k].wait_recv()
             down_pass[k].start()
-
-    @pl.when(has_up)
-    def _():
         for copy in down_pass:
             copy.wait()
 
-    @pl.when(jnp.logical_not(outer))
-    def _():
-        for copy in own_pass:
-            copy.wait()
-
+    for copy in own_pass:
+        copy.wait()
     for k, _ in chunks:
         over_pass[k].wait()
         over[k].wait_send()
@@ -351,32 +331,47 @@
 
 
 def scatter_kernel(
-    near_keep, near_give, far_keep, far_give, from_near, from_far,
-    near_kept, near_got, near_sum, far_kept, far_got, far_sum,
-    nk_sem, fk_sem, ng_send, ng_recv, fg_send, fg_recv, near_send, near_recv, far_send, far_recv,
+    own_keep, own_give, near_keep, near_give, far_keep, far_give, from_near, result,
+    own_kept, own_got, near_kept, near_got, near_sum, far_kept, far_got, far_sum, behind,
+    ok_sem, nk_sem, fk_sem, og_send, og_recv, ng_send, ng_recv, fg_send, fg_recv,
+    near_send, near_recv, far_send, far_recv, out_sem,
 ):
     sibling, across, lower, upper, outer, has_down, has_up = neighbours()
     slices = near_keep.shape[1]
     chunks = list(enumerate((part, layer) for layer in range(slices) for part in range(2)))
-    near_loads = [pltpu.make_async_copy(near_keep.at[p, s], near_kept.at[p, s], nk_sem.at[k]) for k, (p, s) in chunks]
-    far_loads = [pltpu.make_async_copy(far_keep.at[p, s], far_kept.at[p, s], fk_sem.at[k]) for k, (p, s) in chunks]
-    near_gifts = [remote(near_give.at[p, s], near_got.at[p, s], ng_send.at[k], ng_recv.at[k], sibling) for k, (p, s) in chunks]
-    far_gifts = [remote(far_give.at[p, s], far_got.at[p, s], fg_send.at[k], fg_recv.at[k], sibling) for k, (p, s) in chunks]
-    over = [remote(near_sum.at[p, s], from_near.at[p, s], near_send.at[k], near_recv.at[k], across) for k, (p, s) in chunks]
-    up = [remote(far_sum.at[p, s], from_far.at[p, s], far_send.at[k], far_recv.at[k], upper) for k, (p, s) in chunks]
-    hold = [pltpu.make_async_copy(far_sum.at[p, s], from_far.at[p, s], far_send.at[k]) for k, (p, s) in chunks]
-    for k, _ in chunks:
-        near_loads[k].start()
-        far_loads[k].start()
+
+    def load(source, target, sem):
+        return [pltpu.make_async_copy(source.at[p, s], target.at[p, s], sem.at[k]) for k, (p, s) in chunks]
+
+    def give(source, target, send, recv, device):
+        return [remote(source.at[p, s], target.at[p, s], send.at[k], recv.at[k], device) for k, (p, s) in chunks]
+
+    far_loads = load(far_keep, far_kept, fk_sem)
+    near_loads = load(near_keep, near_kept, nk_sem)
+    own_loads = load(own_keep, own_kept, ok_sem)
+    far_gifts = give(far_give, far_got, fg_send, fg_recv, sibling)
+    near_gifts = give(near_give, near_got, ng_send, ng_recv, sibling)
+    own_gifts = give(own_give, own_got, og_send, og_recv, sibling)
+    over = give(near_sum, from_near, near_send, near_recv, across)
+    up = give(far_sum, behind, far_send, far_recv, upper)
+    stores = load(own_kept, result, out_sem)
+    for copies in (far_loads, near_loads, own_loads):
+        for copy in copies:
+            copy.start()
     greet(sibling, across, lower, upper, has_down, has_up)
     for k, _ in chunks:
+        far_gifts[k].start()
         near_gifts[k].start()
-        far_gifts[k].start()
+    for copy in own_gifts:
+        copy.start()
+
+    def send_near(k, extra):
+        p, s = chunks[k][1]
+        total = near_kept[p, s] + near_got[p, s]
+        near_sum[p, s] = total if extra is None else total + extra
+        over[k].start()
+
     for k, (p, s) in chunks:
-        near_loads[k].wait()
-        near_gifts[k].wait_recv()
-        near_sum[p, s] = near_kept[p, s] + near_got[p, s]
-        over[k].start()
         far_loads[k].wait()
         far_gifts[k].wait_recv()
         far_sum[p, s] = far_kept[p, s] + far_got[p, s]
@@ -385,29 +380,52 @@
         def _():
             up[k].start()
 
-        @pl.when(jnp.logical_not(outer))
+        near_loads[k].wait()
+        near_gifts[k].wait_recv()
+
+        @pl.when(outer)
         def _():
-            hold[k].start()
-
+            send_near(k, None)
+
+    inner = jnp.logical_not(outer)
+
+    @pl.when(jnp.logical_and(inner, has_down))
+    def _():
+        for k, (p, s) in chunks:
+            up[k].wait_recv()
+            send_near(k, behind[p, s])
+
+    @pl.when(jnp.logical_and(inner, jnp.logical_not(has_down)))
+    def _():
+        for k, _ in chunks:
+            send_near(k, None)
+
+    for k, (p, s) in chunks:
+        own_loads[k].wait()
+        own_gifts[k].wait_recv()
+        own_kept[p, s] = own_kept[p, s] + own_got[p, s]
+
+    @pl.when(jnp.logical_and(outer, has_down))
+    def _():
+        for k, (p, s) in chunks:
+            up[k].wait_recv()
+            own_kept[p, s] = own_kept[p, s] + behind[p, s]
+
+    for copy in stores:
+        copy.start()
     for k, _ in chunks:
+        far_gifts[k].wait_send()
         near_gifts[k].wait_send()
-        far_gifts[k].wait_send()
+        own_gifts[k].wait_send()
         over[k].wait()
-
-    @pl.when(jnp.logical_not(outer))
-    def _():
-        for copy in hold:
-            copy.wait()
 
     @pl.when(has_up)
     def _():
         for copy in up:
             copy.wait_send()
 
-    @pl.when(has_down)
-    def _():
-        for copy in up:
-            copy.wait_recv()
+    for copy in stores:
+        copy.wait()
 
 
 def local(obj_real, obj_imag, probe, fresnel_phase, row_offset, col_offset, live_count, measured):
@@ -422,56 +440,55 @@
     vmem = pl.BlockSpec(memory_space=pltpu.VMEM)
     anywhere = pl.BlockSpec(memory_space=pl.ANY)
     dma = pltpu.SemaphoreType.DMA
-    near, nearsib, far, farsib = pl.pallas_call(
+    fetched = pl.pallas_call(
         gather_kernel,
-        out_shape=[block] * 4,
+        out_shape=[block] * 5,
         in_specs=[anywhere] * 2,
-        out_specs=[anywhere] * 4,
-        scratch_shapes=[dma((chunks,))] * 8,
+        out_specs=[anywhere] * 5,
+        scratch_shapes=[dma((2,))] * 2 + [dma((chunks,))] * 8,
         compiler_params=pltpu.CompilerParams(
             collective_id=0, has_side_effects=True, vmem_limit_bytes=VMEM_BYTES
         ),
         name="gather_rows",
     )(obj_real, obj_imag)
-    phase = jnp.pad(fresnel_phase, (0, patch - taps)).reshape(1, patch)
+    phase = fresnel_phase.reshape(1, taps)
     dft_left, dft_right = dft_tables(patch)
     parts_of_sum = pl.pallas_call(
         functools.partial(compute_kernel, taps),
-        out_shape=[block] * 4,
-        in_specs=[smem] * 3 + [vmem] * 4 + [anywhere] * 7,
-        out_specs=[anywhere] * 4,
+        out_shape=[block] * 6,
+        in_specs=[smem] * 3 + [vmem] * 4 + [anywhere] * 8,
+        out_specs=[anywhere] * 6,
         scratch_shapes=[
-            pltpu.VMEM((2, slices, parts, 4 * shard, patch), jnp.float32),
-            pltpu.VMEM((2, slices, parts, 4 * shard, patch), jnp.float32),
+            pltpu.VMEM((2, slices, parts, 6 * shard, patch), jnp.float32),
+            pltpu.VMEM((2, slices, parts, 6 * shard, patch), jnp.float32),
             pltpu.VMEM(measured.shape, measured.dtype),
             pltpu.VMEM((2 * patch, 2 * patch), jnp.bfloat16),
             pltpu.VMEM((2 * patch, 2 * patch), jnp.bfloat16),
             pltpu.VMEM((slices - 1, BATCH, 2, patch, patch), jnp.float32),
             pltpu.VMEM((slices - 1, BATCH, 2, patch, patch), jnp.float32),
-            pltpu.SMEM((row_offset.shape[0] + 8,), jnp.int32),
-            pltpu.SemaphoreType.DMA((8 * parts,)),
+            pltpu.VMEM((1, patch), jnp.float32),
+            pltpu.SemaphoreType.DMA((12 * parts,)),
             pltpu.SemaphoreType.DMA,
-            pltpu.SemaphoreType.DMA((8 * parts,)),
+            pltpu.SemaphoreType.DMA((12 * parts,)),
         ],
         compiler_params=pltpu.CompilerParams(vmem_limit_bytes=VMEM_BYTES),
         name="patch_gradients",
     )(
         row_offset, col_offset, live_count, phase, dft_left, dft_right, probe,
-        obj_real, obj_imag, near, nearsib, far, farsib, measured,
+        obj_real, obj_imag, *fetched, measured,
     )
-    from_near, from_far = pl.pallas_call(
+    from_near, rest = pl.pallas_call(
         scatter_kernel,
         out_shape=[block] * 2,
-        in_specs=[anywhere] * 4,
+        in_specs=[anywhere] * 6,
         out_specs=[anywhere] * 2,
-        scratch_shapes=[pltpu.VMEM(block.shape, jnp.float32)] * 6 + [dma((chunks,))] * 10,
+        scratch_shapes=[pltpu.VMEM(block.shape, jnp.float32)] * 9 + [dma((chunks,))] * 14,
         compiler_params=pltpu.CompilerParams(
             collective_id=1, has_side_effects=True, vmem_limit_bytes=VMEM_BYTES
         ),
         name="scatter_rows",
     )(*parts_of_sum)
-    alone = jnp.logical_and(lax.axis_index("tile") == 0, lax.axis_index("pos") < 2)
-    return tuple(from_near[p] + jnp.where(alone, 0.0, from_far[p]) for p in range(2))
+    return tuple(from_near[p] + rest[p] for p in range(2))
 
 
 def solution(mesh):

time: 60.1 us -> 64.8 us (1.078)
  the two profiles are of different devices: /device:TPU:25 before, /device:TPU:24 now
where the time goes in v4:
time: 64.8 us; the launch traced here: 64.7 us
  Pallas kernels  61.3 us (95%)
  other arithmetic  2.05 us (3%)
  between operations  1.3 us (2%)
    pallas_call x1, Pallas kernels, local(): pl.pallas_call(scatter_kernel, out_shape=[block] * 2, in_specs=[anywhere]...  24.6 us
    pallas_call x1, Pallas kernels, local(): pl.pallas_call(functools.partial(compute_kernel, taps), out_shape=[block]...  19.1 us
    pallas_call x1, Pallas kernels, local(): pl.pallas_call(gather_kernel, out_shape=[block] * 5, in_specs=[anywhere]...  17.7 us
    add x1, other arithmetic, local(): return tuple((from_near[p] + rest[p] for p in range(2)))  2.05 us

profile of v4, /device:TPU:24, one launch (start us, length us, event | category | flops | bytes accessed | tf_op | source)
XLA Modules:
  0.0 64.7 jit_solution(11411097678067544456)
XLA Ops:
  1.3 17.7 %gather_rows.1 = (f32[2,4,64,256]{3,2,1,0:T(8,128)}, f32[2,4,64,256]{3,2,1,0:T(8,128)}, f32[2,4,64,256]{3,2,1,0:T(8,128)}, f32[2,4,64,256]{3,2,1,0:T(8,128)}, f32[2,4,64,256]{3,2,1,0:T(8,128)}) custom-call(f32[4,64,256]{2,1,0:T(8,128)} %own_re.1, f32[4,64,256]{2,1,0:T(8,128)} %own_im.1), custom_call_target="tpu_custom_call" | custom-call | tf_op jit(solution)/shard_map/gather_rows/pallas_call | solution.py:443
  18.9 19.1 %patch_gradients.1 = (f32[2,4,64,256]{3,2,1,0:T(8,128)}, f32[2,4,64,256]{3,2,1,0:T(8,128)}, f32[2,4,64,256]{3,2,1,0:T(8,128)}, f32[2,4,64,256]{3,2,1,0:T(8,128)}...) custom-call(s32[64]{0:T(128)} %rows_ref.1, s32[64]{0:T(128)} %cols_ref.1, s32[1]{0:T(128)S(6)} %copy.12.live_ref, ...), custom_call_target="tpu_custom_call" | custom-call | tf_op jit(solution)/shard_map/patch_gradients/pallas_call | solution.py:456
  38.1 24.6 %scatter_rows.1 = (f32[2,4,64,256]{3,2,1,0:T(8,128)}, f32[2,4,64,256]{3,2,1,0:T(8,128)}) custom-call(f32[2,4,64,256]{3,2,1,0:T(8,128)} %get-tuple-element.20.own_keep, f32[2,4,64,256]{3,2,1,0:T(8,128)} %get-tuple-element.21.own_give, f32[2,4,64,256]{3,2,1,0:T(8,128)} %get-tuple-element.22.near_keep, f32[2,4,64,256]{3,2,1,0:T(8,128)} %get-tuple-element.23.near_give, ...), custom_call_target="tpu_custom_call" | custom-call | tf_op jit(solution)/shard_map/scatter_rows/pallas_call | solution.py:480
  62.6 2.0 %add_bitcast_fusion = (f32[4,64,256]{2,1,0:T(8,128)}, f32[4,64,256]{2,1,0:T(8,128)}) fusion(f32[2,4,64,256]{3,2,1,0:T(8,128)} %get-tuple-element.27, f32[2,4,64,256]{3,2,1,0:T(8,128)} %get-tuple-element.26), kind=kLoop, calls=%fused_computation | loop fusion | flops 131072 | bytes 1572864 | tf_op jit(solution)/shard_map/add | solution.py:491

commit v5 on v3

--- a/solution.py
+++ b/solution.py
@@ -10,7 +10,7 @@
 from jax.sharding import PartitionSpec as P
 
 AMP_FLOOR = 0.25
-BATCH = 4
+BATCH = 8
 CHAIN = 2
 VMEM_BYTES = 60 * 1024 * 1024
 
@@ -75,7 +75,7 @@
     taps, rows_ref, cols_ref, live_ref, phase_ref, dft_left, dft_right, probe_ref,
     own_re, own_im, near_ref, nearsib_ref, far_ref, farsib_ref, measured_ref,
     near_keep, near_give, far_keep, far_give,
-    window, acc, target, kern_left, kern_right, saved, patches, listed, in_sem, target_sem, out_sem,
+    window, acc, target, kern_left, kern_right, saved, patches, phases, listed, in_sem, target_sem, out_sem,
 ):
     slices, shard, width = own_re.shape
     patch = probe_ref.shape[-1]
@@ -83,8 +83,10 @@
     parts = width // patch
     member = lax.axis_index("pos")
     parity = member % 2
-    get_target = pltpu.make_async_copy(measured_ref, target, target_sem)
-    get_target.start()
+
+    def get_target(item, slot):
+        return pltpu.make_async_copy(measured_ref.at[slot], target.at[item], target_sem.at[item])
+
     outer = member < 2
     ahead = jnp.logical_and(outer, lax.axis_index("tile") + 1 < lax.axis_size("tile"))
     base = jnp.where(outer, 2 * shard, 0)
@@ -134,6 +136,12 @@
     total = lax.fori_loop(0, slots, pick, jnp.int32(0))
     mine = (total + 1 - parity) // 2
 
+    def fetch(item, carry):
+        get_target(item, listed[item]).start()
+        return carry
+
+    lax.fori_loop(0, mine, fetch, 0)
+
     row = lax.broadcasted_iota(jnp.int32, (patch, patch), 0)
     col = lax.broadcasted_iota(jnp.int32, (patch, patch), 1)
     band = jnp.logical_and(col - row + taps // 2 >= 0, col - row + taps // 2 < taps)
@@ -144,8 +152,10 @@
         moved = pltpu.roll(wide, patch - taps // 2, 1, stride=1, stride_axis=0)
         return jnp.where(band, moved, 0.0)
 
-    kern_re = toeplitz(jnp.cos(phase_ref[...]) * scale)
-    kern_im = toeplitz(jnp.sin(phase_ref[...]) * scale)
+    phases[...] = jnp.zeros_like(phases)
+    phases[:, :taps] = phase_ref[...]
+    kern_re = toeplitz(jnp.cos(phases[...]) * scale)
+    kern_im = toeplitz(jnp.sin(phases[...]) * scale)
     kern_left[...] = stack_rows(halves([(kern_re, kern_im), (-kern_im, kern_re)]))
     kern_re_t, kern_im_t = kern_re.T, kern_im.T
     kern_right[...] = stack_rows(halves([(kern_re_t, -kern_im_t), (kern_im_t, kern_re_t)]))
@@ -158,12 +168,16 @@
         for load in far_loads + farsib_loads:
             load.wait()
 
-    get_target.wait()
-
     def group(first, size):
+        def arrive(item, carry):
+            get_target(item, listed[item]).wait()
+            return carry
+
+        lax.fori_loop(first, jnp.minimum(first + size, mine), arrive, 0)
         every = range(size)
         chains = [list(every)[c : c + CHAIN] for c in range(0, size, CHAIN)]
-        index = [listed[jnp.minimum(first + b, mine - 1)] for b in every]
+        item = [jnp.minimum(first + b, mine - 1) for b in every]
+        index = [listed[i] for i in item]
         weight = [(first + b < mine).astype(jnp.float32) for b in every]
         top = [rows_ref[i] - base for i in index]
         left = [cols_ref[i] for i in index]
@@ -199,7 +213,7 @@
             for b in chain:
                 f_re, f_im = waves[b]
                 amplitude = jnp.sqrt(f_re * f_re + f_im * f_im + AMP_FLOOR)
-                t = target[index[b]].astype(jnp.float32)
+                t = target[item[b]].astype(jnp.float32)
                 ratio = weight[b] * (amplitude - t) / amplitude
                 nxt.append((f_re * ratio, f_im * ratio))
             for b, grad in zip(chain, backward_two_sided(dft_left[...], dft_right[...], nxt)):
@@ -225,7 +239,9 @@
                     for b, grad in zip(chain, backward_two_sided(kern_left[...], kern_right[...], nxt)):
                         grads[b] = grad
 
-    rounds = (mine + BATCH // 2 - 1) // BATCH
+    rounds = (mine + 1) // BATCH
+    rest = mine - rounds * BATCH
+    most = jnp.where(rest > BATCH // 4, BATCH // 2, 0)
 
     def full(step, carry):
         group(step * BATCH, BATCH)
@@ -233,9 +249,13 @@
 
     lax.fori_loop(0, rounds, full, 0)
 
-    @pl.when(rounds * BATCH < mine)
+    @pl.when(most > 0)
     def _():
         group(rounds * BATCH, BATCH // 2)
+
+    @pl.when(rest > most)
+    def _():
+        group(rounds * BATCH + most, BATCH // 4)
 
     stores = []
     for result, spot in zip((near_keep, near_give, far_keep, far_give), spots):
@@ -410,6 +430,12 @@
             copy.wait_recv()
 
 
+def join_kernel(near, far, out_re, out_im):
+    alone = jnp.logical_and(lax.axis_index("tile") == 0, lax.axis_index("pos") < 2)
+    out_re[...] = near[0] + jnp.where(alone, 0.0, far[0])
+    out_im[...] = near[1] + jnp.where(alone, 0.0, far[1])
+
+
 def local(obj_real, obj_imag, probe, fresnel_phase, row_offset, col_offset, live_count, measured):
     slices, shard, width = obj_real.shape
     patch = probe.shape[-1]
@@ -433,7 +459,7 @@
         ),
         name="gather_rows",
     )(obj_real, obj_imag)
-    phase = jnp.pad(fresnel_phase, (0, patch - taps)).reshape(1, patch)
+    phase = fresnel_phase.reshape(1, taps)
     dft_left, dft_right = dft_tables(patch)
     parts_of_sum = pl.pallas_call(
         functools.partial(compute_kernel, taps),
@@ -443,14 +469,15 @@
         scratch_shapes=[
             pltpu.VMEM((2, slices, parts, 4 * shard, patch), jnp.float32),
             pltpu.VMEM((2, slices, parts, 4 * shard, patch), jnp.float32),
-            pltpu.VMEM(measured.shape, measured.dtype),
+            pltpu.VMEM((measured.shape[0] // 2,) + measured.shape[1:], measured.dtype),
             pltpu.VMEM((2 * patch, 2 * patch), jnp.bfloat16),
             pltpu.VMEM((2 * patch, 2 * patch), jnp.bfloat16),
             pltpu.VMEM((slices - 1, BATCH, 2, patch, patch), jnp.float32),
             pltpu.VMEM((slices - 1, BATCH, 2, patch, patch), jnp.float32),
+            pltpu.VMEM((1, patch), jnp.float32),
             pltpu.SMEM((row_offset.shape[0] + 8,), jnp.int32),
             pltpu.SemaphoreType.DMA((8 * parts,)),
-            pltpu.SemaphoreType.DMA,
+            pltpu.SemaphoreType.DMA((measured.shape[0] // 2,)),
             pltpu.SemaphoreType.DMA((8 * parts,)),
         ],
         compiler_params=pltpu.CompilerParams(vmem_limit_bytes=VMEM_BYTES),
@@ -470,8 +497,19 @@
         ),
         name="scatter_rows",
     )(*parts_of_sum)
-    alone = jnp.logical_and(lax.axis_index("tile") == 0, lax.axis_index("pos") < 2)
-    return tuple(from_near[p] + jnp.where(alone, 0.0, from_far[p]) for p in range(2))
+    pair_block = pl.BlockSpec((2, 1, shard, width), lambda layer: (0, layer, 0, 0))
+    one_block = pl.BlockSpec((1, shard, width), lambda layer: (layer, 0, 0))
+    return tuple(
+        pl.pallas_call(
+            join_kernel,
+            out_shape=[jax.ShapeDtypeStruct(obj_real.shape, jnp.float32)] * 2,
+            grid=(slices,),
+            in_specs=[pair_block] * 2,
+            out_specs=[one_block] * 2,
+            compiler_params=pltpu.CompilerParams(vmem_limit_bytes=VMEM_BYTES),
+            name="join_rows",
+        )(from_near, from_far)
+    )
 
 
 def solution(mesh):

time: 60.1 us -> 56.6 us (0.942); the launches traced: 59.8 us -> 55.6 us
  other arithmetic: 2.05 us -> 0 us
  local copies, waits for them, and re-layouts: 1.17 us -> 0 us
  Pallas kernels: 55.3 us -> 54.3 us
    pallas_call x1, Pallas kernels: 22.8 us -> 19.2 us  [local(): pl.pallas_call(scatter_kernel, out_shape=[block] * 2, in_specs=[anywhere]...]
    pallas_call x0 -> x1, Pallas kernels: none -> 3.32 us  [local(): pl.pallas_call(join_kernel, out_shape=[jax.ShapeDtypeStruct(obj_real.shap...]
    add x1 -> x0, other arithmetic: 2.05 us -> none  [local(): from_near[p] + jnp.where(alone, 0.0, from_far[p])]
    reshape x1 -> x0, local copies, waits for them, and re-layouts: 1.17 us -> none  [local(): phase = jnp.pad(fresnel_phase, (0, patch - taps)).reshape(1, patch)]
    pallas_call x1, Pallas kernels: 15.1 us -> 14.3 us  [local(): pl.pallas_call(functools.partial(compute_kernel, taps), out_shape=[block]...]
where the time goes in v5:
time: 56.6 us; the launch traced here: 55.6 us
  Pallas kernels  54.3 us (96%)
  between operations  1.3 us (2%)
    pallas_call x1, Pallas kernels, local(): pl.pallas_call(scatter_kernel, out_shape=[block] * 2, in_specs=[anywhere]...  19.2 us
    pallas_call x1, Pallas kernels, local(): pl.pallas_call(gather_kernel, out_shape=[block] * 4, in_specs=[anywhere]...  17.4 us
    pallas_call x1, Pallas kernels, local(): pl.pallas_call(functools.partial(compute_kernel, taps), out_shape=[block]...  14.3 us
    pallas_call x1, Pallas kernels, local(): pl.pallas_call(join_kernel, out_shape=[jax.ShapeDtypeStruct(obj_real.shap...  3.32 us

profile of v5, /device:TPU:25, one launch (start us, length us, event | category | flops | bytes accessed | tf_op | source)
XLA Modules:
  0.0 55.6 jit_solution(14077901487684056192)
XLA Ops:
  1.3 17.4 %gather_rows.1 = (f32[2,4,64,256]{3,2,1,0:T(8,128)}, f32[2,4,64,256]{3,2,1,0:T(8,128)}, f32[2,4,64,256]{3,2,1,0:T(8,128)}, f32[2,4,64,256]{3,2,1,0:T(8,128)}) custom-call(f32[4,64,256]{2,1,0:T(8,128)} %own_re.1, f32[4,64,256]{2,1,0:T(8,128)} %own_im.1), custom_call_target="tpu_custom_call" | custom-call | tf_op jit(solution)/shard_map/gather_rows/pallas_call | solution.py:451
  18.7 14.3 %patch_gradients.1 = (f32[2,4,64,256]{3,2,1,0:T(8,128)}, f32[2,4,64,256]{3,2,1,0:T(8,128)}, f32[2,4,64,256]{3,2,1,0:T(8,128)}, f32[2,4,64,256]{3,2,1,0:T(8,128)}) custom-call(s32[64]{0:T(128)} %rows_ref.1, s32[64]{0:T(128)} %cols_ref.1, s32[1]{0:T(128)S(6)} %copy.12.live_ref, f32[1,33]{1,0:T(1,128)} %bitcast.1, bf16[256,256]{1,0:T(8,128)(2,1)} %constant.4.clone.dft_left, ...), custom_call_target="tpu_custom_call" | custom-call | tf_op jit(solution)/shard_map/patch_gradients/pallas_call | solution.py:464
  33.0 19.2 %scatter_rows.1 = (f32[2,4,64,256]{3,2,1,0:T(8,128)}, f32[2,4,64,256]{3,2,1,0:T(8,128)}) custom-call(f32[2,4,64,256]{3,2,1,0:T(8,128)} %get-tuple-element.16.near_keep, f32[2,4,64,256]{3,2,1,0:T(8,128)} %get-tuple-element.17.near_give, f32[2,4,64,256]{3,2,1,0:T(8,128)} %get-tuple-element.18.far_keep, f32[2,4,64,256]{3,2,1,0:T(8,128)} %get-tuple-element.19.far_give), custom_call_target="tpu_custom_call" | custom-call | tf_op jit(solution)/shard_map/scatter_rows/pallas_call | solution.py:489
  52.3 3.3 %join_rows.1 = (f32[4,64,256]{2,1,0:T(8,128)}, f32[4,64,256]{2,1,0:T(8,128)}) custom-call(f32[2,4,64,256]{3,2,1,0:T(8,128)} %get-tuple-element.20.near, f32[2,4,64,256]{3,2,1,0:T(8,128)} %get-tuple-element.21.far), custom_call_target="tpu_custom_call" | custom-call | tf_op jit(solution)/shard_map/join_rows/pallas_call | solution.py:503

commit v6 on v5

--- a/solution.py
+++ b/solution.py
@@ -75,7 +75,7 @@
     taps, rows_ref, cols_ref, live_ref, phase_ref, dft_left, dft_right, probe_ref,
     own_re, own_im, near_ref, nearsib_ref, far_ref, farsib_ref, measured_ref,
     near_keep, near_give, far_keep, far_give,
-    window, acc, target, kern_left, kern_right, saved, patches, phases, listed, in_sem, target_sem, out_sem,
+    window, acc, target, kern_left, kern_right, saved, phases, listed, in_sem, target_sem, out_sem,
 ):
     slices, shard, width = own_re.shape
     patch = probe_ref.shape[-1]
@@ -198,8 +198,6 @@
                     o_re, o_im = cut(layer, b, 0), cut(layer, b, 1)
                     w_re, w_im = waves[b]
                     if layer:
-                        patches[layer - 1, b, 0] = o_re
-                        patches[layer - 1, b, 1] = o_im
                         saved[layer - 1, b, 0] = w_re
                         saved[layer - 1, b, 1] = w_im
                     nxt.append((w_re * o_re - w_im * o_im, w_re * o_im + w_im * o_re))
@@ -212,9 +210,9 @@
             nxt = []
             for b in chain:
                 f_re, f_im = waves[b]
-                amplitude = jnp.sqrt(f_re * f_re + f_im * f_im + AMP_FLOOR)
+                inverse = lax.rsqrt(f_re * f_re + f_im * f_im + AMP_FLOOR)
                 t = target[item[b]].astype(jnp.float32)
-                ratio = weight[b] * (amplitude - t) / amplitude
+                ratio = weight[b] * (1.0 - t * inverse)
                 nxt.append((f_re * ratio, f_im * ratio))
             for b, grad in zip(chain, backward_two_sided(dft_left[...], dft_right[...], nxt)):
                 grads[b] = grad
@@ -225,7 +223,7 @@
                     g_re, g_im = grads[b]
                     if layer:
                         w_re, w_im = saved[layer - 1, b, 0], saved[layer - 1, b, 1]
-                        o_re, o_im = patches[layer - 1, b, 0], patches[layer - 1, b, 1]
+                        o_re, o_im = cut(layer, b, 0), cut(layer, b, 1)
                         nxt.append((o_re * g_re + o_im * g_im, o_re * g_im - o_im * g_re))
                     else:
                         w_re, w_im = probe_ref[0], probe_ref[1]
@@ -428,12 +426,6 @@
     def _():
         for copy in up:
             copy.wait_recv()
-
-
-def join_kernel(near, far, out_re, out_im):
-    alone = jnp.logical_and(lax.axis_index("tile") == 0, lax.axis_index("pos") < 2)
-    out_re[...] = near[0] + jnp.where(alone, 0.0, far[0])
-    out_im[...] = near[1] + jnp.where(alone, 0.0, far[1])
 
 
 def local(obj_real, obj_imag, probe, fresnel_phase, row_offset, col_offset, live_count, measured):
@@ -473,7 +465,6 @@
             pltpu.VMEM((2 * patch, 2 * patch), jnp.bfloat16),
             pltpu.VMEM((2 * patch, 2 * patch), jnp.bfloat16),
             pltpu.VMEM((slices - 1, BATCH, 2, patch, patch), jnp.float32),
-            pltpu.VMEM((slices - 1, BATCH, 2, patch, patch), jnp.float32),
             pltpu.VMEM((1, patch), jnp.float32),
             pltpu.SMEM((row_offset.shape[0] + 8,), jnp.int32),
             pltpu.SemaphoreType.DMA((8 * parts,)),
@@ -497,19 +488,8 @@
         ),
         name="scatter_rows",
     )(*parts_of_sum)
-    pair_block = pl.BlockSpec((2, 1, shard, width), lambda layer: (0, layer, 0, 0))
-    one_block = pl.BlockSpec((1, shard, width), lambda layer: (layer, 0, 0))
-    return tuple(
-        pl.pallas_call(
-            join_kernel,
-            out_shape=[jax.ShapeDtypeStruct(obj_real.shape, jnp.float32)] * 2,
-            grid=(slices,),
-            in_specs=[pair_block] * 2,
-            out_specs=[one_block] * 2,
-            compiler_params=pltpu.CompilerParams(vmem_limit_bytes=VMEM_BYTES),
-            name="join_rows",
-        )(from_near, from_far)
-    )
+    alone = jnp.logical_and(lax.axis_index("tile") == 0, lax.axis_index("pos") < 2)
+    return tuple(from_near[p] + jnp.where(alone, 0.0, from_far[p]) for p in range(2))
 
 
 def solution(mesh):

time: 56.6 us -> 55.9 us (0.988)
  the two profiles are of different devices: /device:TPU:25 before, /device:TPU:16 now
where the time goes in v6:
time: 55.9 us; the launch traced here: 55.6 us
  Pallas kernels  52.2 us (93%)
  other arithmetic  2.05 us (4%)
  between operations  1.31 us (2%)
    pallas_call x1, Pallas kernels, local(): pl.pallas_call(functools.partial(compute_kernel, taps), out_shape=[block]...  17.8 us
    pallas_call x1, Pallas kernels, local(): pl.pallas_call(scatter_kernel, out_shape=[block] * 2, in_specs=[anywhere]...  17.5 us
    pallas_call x1, Pallas kernels, local(): pl.pallas_call(gather_kernel, out_shape=[block] * 4, in_specs=[anywhere]...  16.9 us
    add x1, other arithmetic, local(): from_near[p] + jnp.where(alone, 0.0, from_far[p])  2.05 us

profile of v6, /device:TPU:16, one launch (start us, length us, event | category | flops | bytes accessed | tf_op | source)
XLA Modules:
  0.0 55.6 jit_solution(5165253151512646040)
XLA Ops:
  0.6 16.9 %gather_rows.1 = (f32[2,4,64,256]{3,2,1,0:T(8,128)}, f32[2,4,64,256]{3,2,1,0:T(8,128)}, f32[2,4,64,256]{3,2,1,0:T(8,128)}, f32[2,4,64,256]{3,2,1,0:T(8,128)}) custom-call(f32[4,64,256]{2,1,0:T(8,128)} %own_re.1, f32[4,64,256]{2,1,0:T(8,128)} %own_im.1), custom_call_target="tpu_custom_call" | custom-call | tf_op jit(solution)/shard_map/gather_rows/pallas_call | solution.py:443
  18.2 17.8 %patch_gradients.1 = (f32[2,4,64,256]{3,2,1,0:T(8,128)}, f32[2,4,64,256]{3,2,1,0:T(8,128)}, f32[2,4,64,256]{3,2,1,0:T(8,128)}, f32[2,4,64,256]{3,2,1,0:T(8,128)}) custom-call(s32[64]{0:T(128)} %rows_ref.1, s32[64]{0:T(128)} %cols_ref.1, s32[1]{0:T(128)S(6)} %copy.12.live_ref, f32[1,33]{1,0:T(1,128)} %bitcast.5, bf16[256,256]{1,0:T(8,128)(2,1)} %constant.19.clone.dft_left, ...), custom_call_target="tpu_custom_call" | custom-call | tf_op jit(solution)/shard_map/patch_gradients/pallas_call | solution.py:456
  36.0 17.5 %scatter_rows.1 = (f32[2,4,64,256]{3,2,1,0:T(8,128)}, f32[2,4,64,256]{3,2,1,0:T(8,128)}) custom-call(f32[2,4,64,256]{3,2,1,0:T(8,128)} %get-tuple-element.16.near_keep, f32[2,4,64,256]{3,2,1,0:T(8,128)} %get-tuple-element.17.near_give, f32[2,4,64,256]{3,2,1,0:T(8,128)} %get-tuple-element.18.far_keep, f32[2,4,64,256]{3,2,1,0:T(8,128)} %get-tuple-element.19.far_give), custom_call_target="tpu_custom_call" | custom-call | tf_op jit(solution)/shard_map/scatter_rows/pallas_call | solution.py:480
  53.5 2.0 %add_bitcast_fusion = (f32[4,64,256]{2,1,0:T(8,128)}, f32[4,64,256]{2,1,0:T(8,128)}) fusion(f32[2,4,64,256]{3,2,1,0:T(8,128)} %get-tuple-element.21, f32[2,4,64,256]{3,2,1,0:T(8,128)} %get-tuple-element.20, pred[]{:T(512)S(6)} %and.5), kind=kLoop, calls=%fused_computation | loop fusion | flops 262144 | bytes 1572865 | tf_op jit(solution)/shard_map/add | solution.py:492

commit v7 on v6

--- a/solution.py
+++ b/solution.py
@@ -10,7 +10,7 @@
 from jax.sharding import PartitionSpec as P
 
 AMP_FLOOR = 0.25
-BATCH = 8
+BATCH = 4
 CHAIN = 2
 VMEM_BYTES = 60 * 1024 * 1024
 
@@ -382,6 +382,7 @@
     far_gifts = [remote(far_give.at[p, s], far_got.at[p, s], fg_send.at[k], fg_recv.at[k], sibling) for k, (p, s) in chunks]
     over = [remote(near_sum.at[p, s], from_near.at[p, s], near_send.at[k], near_recv.at[k], across) for k, (p, s) in chunks]
     up = [remote(far_sum.at[p, s], from_far.at[p, s], far_send.at[k], far_recv.at[k], upper) for k, (p, s) in chunks]
+    blank = [pltpu.make_async_copy(near_kept.at[p, s], from_far.at[p, s], nk_sem.at[k]) for k, (p, s) in chunks]
     hold = [pltpu.make_async_copy(far_sum.at[p, s], from_far.at[p, s], far_send.at[k]) for k, (p, s) in chunks]
     for k, _ in chunks:
         near_loads[k].start()
@@ -406,6 +407,14 @@
         @pl.when(jnp.logical_not(outer))
         def _():
             hold[k].start()
+
+    @pl.when(jnp.logical_and(outer, jnp.logical_not(has_down)))
+    def _():
+        near_kept[...] = jnp.zeros_like(near_kept)
+        for copy in blank:
+            copy.start()
+        for copy in blank:
+            copy.wait()
 
     for k, _ in chunks:
         near_gifts[k].wait_send()
@@ -488,8 +497,7 @@
         ),
         name="scatter_rows",
     )(*parts_of_sum)
-    alone = jnp.logical_and(lax.axis_index("tile") == 0, lax.axis_index("pos") < 2)
-    return tuple(from_near[p] + jnp.where(alone, 0.0, from_far[p]) for p in range(2))
+    return tuple(from_near[p] + from_far[p] for p in range(2))
 
 
 def solution(mesh):

time: 55.9 us -> 58 us (1.038)
  the two profiles are of different devices: /device:TPU:16 before, /device:TPU:9 now
where the time goes in v7:
time: 58 us; the launch traced here: 57.5 us
  Pallas kernels  54.1 us (93%)
  other arithmetic  2.05 us (4%)
  between operations  1.3 us (2%)
    pallas_call x1, Pallas kernels, local(): pl.pallas_call(scatter_kernel, out_shape=[block] * 2, in_specs=[anywhere]...  24.6 us
    pallas_call x1, Pallas kernels, local(): pl.pallas_call(gather_kernel, out_shape=[block] * 4, in_specs=[anywhere]...  17.4 us
    pallas_call x1, Pallas kernels, local(): pl.pallas_call(functools.partial(compute_kernel, taps), out_shape=[block]...  12.1 us
    add x1, other arithmetic, local(): return tuple((from_near[p] + from_far[p] for p in range(2)))  2.05 us

profile of v7, /device:TPU:9, one launch (start us, length us, event | category | flops | bytes accessed | tf_op | source)
XLA Modules:
  0.0 57.5 jit_solution(4990525350558681619)
XLA Ops:
  1.3 17.4 %gather_rows.1 = (f32[2,4,64,256]{3,2,1,0:T(8,128)}, f32[2,4,64,256]{3,2,1,0:T(8,128)}, f32[2,4,64,256]{3,2,1,0:T(8,128)}, f32[2,4,64,256]{3,2,1,0:T(8,128)}) custom-call(f32[4,64,256]{2,1,0:T(8,128)} %own_re.1, f32[4,64,256]{2,1,0:T(8,128)} %own_im.1), custom_call_target="tpu_custom_call" | custom-call | tf_op jit(solution)/shard_map/gather_rows/pallas_call | solution.py:452
  18.7 12.1 %patch_gradients.1 = (f32[2,4,64,256]{3,2,1,0:T(8,128)}, f32[2,4,64,256]{3,2,1,0:T(8,128)}, f32[2,4,64,256]{3,2,1,0:T(8,128)}, f32[2,4,64,256]{3,2,1,0:T(8,128)}) custom-call(s32[64]{0:T(128)} %rows_ref.1, s32[64]{0:T(128)} %cols_ref.1, s32[1]{0:T(128)S(6)} %copy.12.live_ref, f32[1,33]{1,0:T(1,128)} %bitcast.5, bf16[256,256]{1,0:T(8,128)(2,1)} %constant.4.clone.dft_left, ...), custom_call_target="tpu_custom_call" | custom-call | tf_op jit(solution)/shard_map/patch_gradients/pallas_call | solution.py:465
  30.8 24.6 %scatter_rows.1 = (f32[2,4,64,256]{3,2,1,0:T(8,128)}, f32[2,4,64,256]{3,2,1,0:T(8,128)}) custom-call(f32[2,4,64,256]{3,2,1,0:T(8,128)} %get-tuple-element.16.near_keep, f32[2,4,64,256]{3,2,1,0:T(8,128)} %get-tuple-element.17.near_give, f32[2,4,64,256]{3,2,1,0:T(8,128)} %get-tuple-element.18.far_keep, f32[2,4,64,256]{3,2,1,0:T(8,128)} %get-tuple-element.19.far_give), custom_call_target="tpu_custom_call" | custom-call | tf_op jit(solution)/shard_map/scatter_rows/pallas_call | solution.py:489
  55.4 2.0 %add_bitcast_fusion = (f32[4,64,256]{2,1,0:T(8,128)}, f32[4,64,256]{2,1,0:T(8,128)}) fusion(f32[2,4,64,256]{3,2,1,0:T(8,128)} %get-tuple-element.21, f32[2,4,64,256]{3,2,1,0:T(8,128)} %get-tuple-element.20), kind=kLoop, calls=%fused_computation | loop fusion | flops 131072 | bytes 1572864 | tf_op jit(solution)/shard_map/add | solution.py:500
